TPU v7x, 128 devices: a whole 4x4x4 slice. The times are simulated.
128 devices in a mesh: blk: 32 (over y_lo, z, x), dp: 4 (over y_hi, core).
Axes of the slice: x: 4, y: 4 (y_hi: 2, y_lo: 2; y = y_hi * 2 + y_lo), z: 4, core: 2. Of those that a mesh axis runs over, the one named last changes fastest.
Arguments:
- hidden_rows: bfloat16 [4096, 4, 5376], P('blk'), may hold values from -320 to 320
- head_weight: bfloat16 [131072, 5376], P(('blk', 'dp')), may hold values from -1 to 1
- targets: int32 [4096], P('blk'), may hold values from 0 to 131071, as said below
Outputs:
- cross_entropy: float32 [4096, 4], P('blk')
- divergence: float32 [4096, 3], P('blk')
Inputs may be any that keep to these rules, and one draw needn't show every extreme that they name: targets[t] = ((t // 128) * 4096 + o) mod 131072 for some o with 0 <= o < 16384.
All inputs are finite; a program needn't handle non-finite values.
Results may differ from a plain program's by a relative error of at most 0.0003.
Values may be sent and summed in bfloat16 or wider, within the bound.
No kernel may reach another device: no remote copies, remote signals or barrier semaphores. Data moves between devices by JAX's collectives and lax.ppermute only.
A program may use at most 128 MiB of HBM per device.

v0:
```python
import jax
import jax.numpy as jnp
from jax import lax
from jax.sharding import PartitionSpec as P

STEPS = 4


def shifted(value, axis, by):
    devices = lax.axis_size(axis)
    return lax.ppermute(value, axis, [(i, (i + by) % devices) for i in range(devices)])


def combined_all(value, axis, join):
    pieces = jax.tree.map(lambda part: lax.all_gather(part, axis), value)
    head = jax.tree.map(lambda part: part[0], pieces)
    tail = jax.tree.map(lambda part: part[1:], pieces)
    running, _ = lax.scan(lambda running, slab: (join(running, slab), None), head, tail)
    return running


def block_summary(row_block, head_block, wanted, vocab_start):
    row_count = row_block.shape[0]
    vocab_count = head_block.shape[0]
    flattened = row_block.reshape(row_count * 4, row_block.shape[2])
    logits = lax.dot_general(
        flattened, head_block, (((1,), (1,)), ((), ())), preferred_element_type=jnp.float32
    )
    logits = logits.reshape(row_count, 4, vocab_count)
    peak = jnp.max(logits, axis=2)
    scaled = jnp.exp(logits - peak[:, :, None])
    total = jnp.sum(scaled, axis=2)
    spread = jnp.sum(scaled[:, 3:4, :] * (logits[:, 3:4, :] - logits), axis=2)
    vocab_ids = vocab_start + lax.iota(jnp.int32, vocab_count)
    chosen = vocab_ids[None, None, :] == wanted[:, None, None]
    target_logit = jnp.sum(jnp.where(chosen, logits, 0.0), axis=2)
    return (peak, total, spread, target_logit)


def combine_summary(first, second):
    peak = jnp.maximum(first[0], second[0])
    first_weight = jnp.exp(first[0] - peak)
    second_weight = jnp.exp(second[0] - peak)
    total = first[1] * first_weight + second[1] * second_weight
    spread = first[2] * first_weight[:, 3:4] + second[2] * second_weight[:, 3:4]
    return (peak, total, spread, first[3] + second[3])


def on_device(hidden_rows, head_weight, targets):
    vocab_count = head_weight.shape[0]
    blocks = lax.axis_size("blk")
    dp_count = lax.axis_size("dp")
    place = lax.axis_index("blk")
    column = lax.axis_index("dp")

    def vocab_start(owner):
        return (owner % blocks * dp_count + column) * vocab_count

    summary = block_summary(hidden_rows, head_weight, targets, vocab_start(place))
    current = hidden_rows
    current_wanted = targets
    for distance in range(1, STEPS):
        current = shifted(current, "blk", 1)
        current_wanted = shifted(current_wanted, "blk", 1)
        summary = shifted((summary[0], summary[1], summary[2], summary[3]), "blk", 1)
        summary = combine_summary(
            summary, block_summary(current, head_weight, current_wanted, vocab_start(place))
        )
    summary = shifted((summary[0], summary[1], summary[2], summary[3]), "blk", 1 - STEPS)
    summary = combined_all((summary[0], summary[1], summary[2], summary[3]), "dp", combine_summary)
    peak, total, spread, target_logit = summary
    log_total = peak + jnp.log(total)
    cross_entropy = log_total - target_logit
    divergence = spread[:, :3] / total[:, 3:4] - log_total[:, 3:4] + log_total[:, :3]
    return (cross_entropy, divergence)


def solution(mesh):
    in_specs = (P("blk", None, None), P(("blk", "dp"), None), P("blk"))
    out_specs = (P("blk", None), P("blk", None))
    return jax.shard_map(
        on_device, mesh=mesh, in_specs=in_specs, out_specs=out_specs, check_vma=False
    )
```

profile of v0, /device:TPU:1, one launch (start us, length us, event | category | flops | bytes accessed | tf_op | source)
XLA Modules:
  0.0 438.6 jit_solution(12945280054352080314)
XLA Ops:
  0.6 3.3 copy.5
  3.9 2.1 collective-permute-start.1
  6.0 124.2 %collective-permute-done.1 = bf16[128,4,5376]{2,0,1:T(8,128)(2,1)} collective-permute-done((bf16[128,4,5376]{2,0,1:T(8,128)(2,1)S(1)}, bf16[128,4,5376]{2,0,1:T(8,128)(2,1)}, u32[]{:S(2)}, u32[]{:S(2)}) %collective-permute-start.1) | collective-permute-done | bytes 5505056 | tf_op jit(solution)/shard_map/ppermute | solution.py:11
  130.3 8.8 %fusion.21 = (f32[128,4]{0,1:T(4,128)S(1)}, f32[128,4,1024]{2,0,1:T(8,128)S(1)}) fusion(bf16[1024,5376]{1,0:T(8,128)(2,1)} %param.6, bf16[128,4,5376]{2,1,0:T(4,128)(2,1)S(1)} %copy-done), kind=kOutput, calls=%fused_computation.79 | convolution fusion | flops 5637668352 | bytes 18614272 | tf_op jit(solution)/shard_map/dot_general | solution.py:26
  139.2 1.8 fusion.14
  140.9 1.1 collective-permute-start.7
  142.1 1.1 slice_bitcast_fusion.9
  143.2 110.5 %collective-permute-done.16 = s32[128]{0:T(128)S(1)} collective-permute-done((s32[128]{0:T(128)S(1)}, s32[128]{0:T(128)S(1)}, u32[]{:S(2)}, u32[]{:S(2)}) %collective-permute-start.16) | collective-permute-done | bytes 544 | tf_op jit(solution)/shard_map/ppermute | solution.py:11
  253.7 6.6 %collective-permute-done.18 = s32[128]{0:T(128)S(1)} collective-permute-done((s32[128]{0:T(128)S(1)}, s32[128]{0:T(128)S(1)}, u32[]{:S(2)}, u32[]{:S(2)}) %collective-permute-start.18) | collective-permute-done | bytes 544 | tf_op jit(solution)/shard_map/ppermute | solution.py:11
  260.3 6.6 %collective-permute-done.20 = s32[128]{0:T(128)S(1)} collective-permute-done((s32[128]{0:T(128)S(1)}, s32[128]{0:T(128)S(1)}, u32[]{:S(2)}, u32[]{:S(2)}) %collective-permute-start.20) | collective-permute-done | bytes 544 | tf_op jit(solution)/shard_map/ppermute | solution.py:11
  266.9 0.4 broadcast_compare_fusion.3
  267.3 0.7 select_reduce_fusion.3
  268.3 10.9 %fusion.20 = (f32[128,4]{0,1:T(4,128)S(1)}, f32[128,4,1024]{2,0,1:T(8,128)S(1)}) fusion(bf16[128,4,5376]{2,0,1:T(8,128)(2,1)} %collective-permute-done.1, bf16[1024,5376]{1,0:T(8,128)(2,1)} %param.6), kind=kOutput, calls=%fused_computation.78 | convolution fusion | flops 5637668352 | bytes 18614272 | tf_op jit(solution)/shard_map/dot_general | solution.py:26
  279.2 0.5 fusion.15
  279.9 0.1 slice_bitcast_fusion.6
  280.0 0.6 select_reduce_fusion.2
  280.6 0.3 collective-permute-start.17
  281.0 8.0 %fusion.19 = (f32[128,4]{0,1:T(4,128)S(1)}, f32[128,4,1024]{2,0,1:T(8,128)S(1)}) fusion(bf16[128,4,5376]{2,0,1:T(8,128)(2,1)} %collective-permute-done.3, bf16[1024,5376]{1,0:T(8,128)(2,1)S(1)} %bitcast.90), kind=kOutput, calls=%fused_computation.77 | convolution fusion | flops 5637668352 | bytes 18614272 | tf_op jit(solution)/shard_map/dot_general | solution.py:26
  289.0 0.5 fusion.16
  289.5 99.0 %collective-permute-done.8 = f32[128,4]{0,1:T(4,128)S(1)} collective-permute-done((f32[128,4]{0,1:T(4,128)S(1)}, f32[128,4]{0,1:T(4,128)S(1)}, u32[]{:S(2)}, u32[]{:S(2)}) %collective-permute-start.8) | collective-permute-done | bytes 2080 | tf_op jit(solution)/shard_map/ppermute | solution.py:11
  388.8 0.6 select_reduce_fusion.1
  389.6 5.9 %fusion.18 = (f32[128,4]{0,1:T(4,128)S(1)}, f32[128,4,1024]{2,0,1:T(8,128)S(1)}) fusion(bf16[128,4,5376]{2,0,1:T(8,128)(2,1)S(1)} %collective-permute-done.5, bf16[1024,5376]{1,0:T(8,128)(2,1)S(1)} %bitcast.90), kind=kOutput, calls=%fused_computation.76 | convolution fusion | flops 5637668352 | bytes 18614272 | tf_op jit(solution)/shard_map/dot_general | solution.py:26
  395.6 0.5 fusion.17
  396.1 6.5 %collective-permute-start.10 = (f32[128,4]{0,1:T(4,128)S(1)}, f32[128,4]{0,1:T(4,128)S(1)}, u32[]{:S(2)}, u32[]{:S(2)}) collective-permute-start(f32[128,4]{0,1:T(4,128)S(1)} %get-tuple-element.88), channel_id=1, source_target_pairs={{0,116},{4,120},{8,124},{12,0},{16,4},{20,8},{24,12},{28,16},{32,2... | collective-permute-start | bytes 6152 | tf_op jit(solution)/shard_map/ppermute | solution.py:11
  402.8 0.6 select_reduce_fusion
  403.7 13.5 %all-gather.1 = f32[512,4]{0,1:T(4,128)S(1)} all-gather(f32[128,4]{0,1:T(4,128)S(1)} %collective-permute-done.10), channel_id=3, replica_groups=mesh['blk'=32,'dp'=4] {'dp'}, dimensions={0}, use_global_device_ids=true | all-gather | bytes 10240 | tf_op jit(solution)/shard_map/all_gather | solution.py:15
  417.2 6.7 %all-gather = f32[512,4]{0,1:T(4,128)S(1)} all-gather(f32[128,4]{0,1:T(4,128)S(1)} %collective-permute-done.6), channel_id=2, replica_groups=mesh['blk'=32,'dp'=4] {'dp'}, dimensions={0}, use_global_device_ids=true | all-gather | bytes 10240 | tf_op jit(solution)/shard_map/all_gather | solution.py:15
  423.8 6.7 %all-gather.3 = f32[512,4]{0,1:T(4,128)S(1)} all-gather(f32[128,4]{0,1:T(4,128)S(1)} %collective-permute-done.21), channel_id=5, replica_groups=mesh['blk'=32,'dp'=4] {'dp'}, dimensions={0}, use_global_device_ids=true | all-gather | bytes 10240 | tf_op jit(solution)/shard_map/all_gather | solution.py:15
  430.5 6.7 %all-gather.2 = f32[512,4]{0,1:T(4,128)S(1)} all-gather(f32[128,4]{0,1:T(4,128)S(1)} %collective-permute-done.14), channel_id=4, replica_groups=mesh['blk'=32,'dp'=4] {'dp'}, dimensions={0}, use_global_device_ids=true | all-gather | bytes 10240 | tf_op jit(solution)/shard_map/all_gather | solution.py:15
  437.2 0.2 while.16
  437.4 0.6 fusion.13
  438.0 0.6 slice_add_fusion
  (84 shorter events, 1.7 us)
Async XLA Ops:
  0.6 129.6 %copy-start = (bf16[128,4,5376]{2,1,0:T(4,128)(2,1)S(1)}, bf16[128,4,5376]{2,1,0:T(4,128)(2,1)}, u32[]{:S(2)}) copy-start(bf16[128,4,5376]{2,1,0:T(4,128)(2,1)} %param.5) | copy-start | bytes 16515076
  0.6 129.6 %copy-start.1 = (s32[128]{0:T(128)S(1)}, s32[128]{0:T(128)}, u32[]{:S(2)}) copy-start(s32[128]{0:T(128)} %param.7) | copy-start | bytes 1540
  3.9 126.4 %collective-permute-start.1 = (bf16[128,4,5376]{2,0,1:T(8,128)(2,1)S(1)}, bf16[128,4,5376]{2,0,1:T(8,128)(2,1)}, u32[]{:S(2)}, u32[]{:S(2)}) collective-permute-start(bf16[128,4,5376]{2,0,1:T(8,128)(2,1)S(1)} %copy.5), channel_id=1, source_target_pairs={{0,4},{4,8},{8,12},{12,16},{16,20},{20,24},{24,28},{28,32},{32,36}... | collective-permute-start | bytes 16515080 | tf_op jit(solution)/shard_map/ppermute | solution.py:11
  130.3 137.9 %collective-permute-start.3 = (bf16[128,4,5376]{2,0,1:T(8,128)(2,1)}, bf16[128,4,5376]{2,0,1:T(8,128)(2,1)}, u32[]{:S(2)}, u32[]{:S(2)}) collective-permute-start(bf16[128,4,5376]{2,0,1:T(8,128)(2,1)} %collective-permute-done.1), channel_id=1, source_target_pairs={{0,4},{4,8},{8,12},{12,16},{16,20},{20,24},{24,28},{28,32},{32,36}... | collective-permute-start | bytes 16515080 | tf_op jit(solution)/shard_map/ppermute | solution.py:11
  130.3 123.5 %collective-permute-start.16 = (s32[128]{0:T(128)S(1)}, s32[128]{0:T(128)S(1)}, u32[]{:S(2)}, u32[]{:S(2)}) collective-permute-start(s32[128]{0:T(128)S(1)} %copy-done.1), channel_id=1, source_target_pairs={{0,4},{4,8},{8,12},{12,16},{16,20},{20,24},{24,28},{28,32},{32,36}... | collective-permute-start | bytes 1544 | tf_op jit(solution)/shard_map/ppermute | solution.py:11
  139.1 140.6 %collective-permute-start = (f32[128,4]{0,1:T(4,128)S(1)}, f32[128,4]{0,1:T(4,128)S(1)}, u32[]{:S(2)}, u32[]{:S(2)}) collective-permute-start(f32[128,4]{0,1:T(4,128)S(1)} %get-tuple-element.120), channel_id=1, source_target_pairs={{0,4},{4,8},{8,12},{12,16},{16,20},{20,24},{24,28},{28,32},{32,36}... | collective-permute-start | bytes 6152 | tf_op jit(solution)/shard_map/ppermute | solution.py:11
  140.9 138.7 %collective-permute-start.7 = (f32[128,4]{0,1:T(4,128)S(1)}, f32[128,4]{0,1:T(4,128)S(1)}, u32[]{:S(2)}, u32[]{:S(2)}) collective-permute-start(f32[128,4]{0,1:T(4,128)S(1)} %get-tuple-element.100), channel_id=1, source_target_pairs={{0,4},{4,8},{8,12},{12,16},{16,20},{20,24},{24,28},{28,32},{32,36}... | collective-permute-start | bytes 6152 | tf_op jit(solution)/shard_map/ppermute | solution.py:11
  253.7 6.6 %collective-permute-start.18 = (s32[128]{0:T(128)S(1)}, s32[128]{0:T(128)S(1)}, u32[]{:S(2)}, u32[]{:S(2)}) collective-permute-start(s32[128]{0:T(128)S(1)} %collective-permute-done.16), channel_id=1, source_target_pairs={{0,4},{4,8},{8,12},{12,16},{16,20},{20,24},{24,28},{28,32},{32,36}... | collective-permute-start | bytes 1544 | tf_op jit(solution)/shard_map/ppermute | solution.py:11
  260.3 6.6 %collective-permute-start.20 = (s32[128]{0:T(128)S(1)}, s32[128]{0:T(128)S(1)}, u32[]{:S(2)}, u32[]{:S(2)}) collective-permute-start(s32[128]{0:T(128)S(1)} %collective-permute-done.18), channel_id=1, source_target_pairs={{0,4},{4,8},{8,12},{12,16},{16,20},{20,24},{24,28},{28,32},{32,36}... | collective-permute-start | bytes 1544 | tf_op jit(solution)/shard_map/ppermute | solution.py:11
  267.3 13.7 %slice-start = ((s8[11010048]{0:T(1024)(128)(4,1)}), s8[4194304]{0:T(1024)(128)(4,1)S(1)}, s32[]{:S(2)}) async-start(s8[11010048]{0:T(1024)(128)(4,1)} %bitcast.89), calls=%async_computation | async-start | bytes 8388608
  268.0 12.6 %collective-permute-start.15 = (f32[128,4]{0,1:T(4,128)S(1)}, f32[128,4]{0,1:T(4,128)S(1)}, u32[]{:S(2)}, u32[]{:S(2)}) collective-permute-start(f32[128,4]{0,1:T(4,128)S(1)} %get-tuple-element.62), channel_id=1, source_target_pairs={{0,4},{4,8},{8,12},{12,16},{16,20},{20,24},{24,28},{28,32},{32,36}... | collective-permute-start | bytes 6152 | tf_op jit(solution)/shard_map/ppermute | solution.py:11
  268.1 12.9 %slice-start.1 = ((s8[11010048]{0:T(1024)(128)(4,1)}), s8[4194304]{0:T(1024)(128)(4,1)S(1)}, s32[]{:S(2)}) async-start(s8[11010048]{0:T(1024)(128)(4,1)} %bitcast.89), calls=%async_computation.1 | async-start | bytes 8388608
  268.1 12.9 %slice-start.2 = ((s8[11010048]{0:T(1024)(128)(4,1)}), s8[2621440]{0:T(1024)(128)(4,1)S(1)}, s32[]{:S(2)}) async-start(s8[11010048]{0:T(1024)(128)(4,1)} %bitcast.89), calls=%async_computation.2 | async-start | bytes 5242880
  268.1 12.8 %collective-permute-start.11 = (f32[128,4]{0,1:T(4,128)S(1)}, f32[128,4]{0,1:T(4,128)S(1)}, u32[]{:S(2)}, u32[]{:S(2)}) collective-permute-start(f32[128,4]{0,1:T(4,128)S(1)} %get-tuple-element.63), channel_id=1, source_target_pairs={{0,4},{4,8},{8,12},{12,16},{16,20},{20,24},{24,28},{28,32},{32,36}... | collective-permute-start | bytes 6152 | tf_op jit(solution)/shard_map/ppermute | solution.py:11
  268.2 121.4 %collective-permute-start.5 = (bf16[128,4,5376]{2,0,1:T(8,128)(2,1)}, bf16[128,4,5376]{2,0,1:T(8,128)(2,1)S(1)}, u32[]{:S(2)}, u32[]{:S(2)}) collective-permute-start(bf16[128,4,5376]{2,0,1:T(8,128)(2,1)} %collective-permute-done.3), channel_id=1, source_target_pairs={{0,4},{4,8},{8,12},{12,16},{16,20},{20,24},{24,28},{28,32},{32,36}... | collective-permute-start | bytes 16515080 | tf_op jit(solution)/shard_map/ppermute | solution.py:11
  279.7 108.8 %collective-permute-start.8 = (f32[128,4]{0,1:T(4,128)S(1)}, f32[128,4]{0,1:T(4,128)S(1)}, u32[]{:S(2)}, u32[]{:S(2)}) collective-permute-start(f32[128,4]{0,1:T(4,128)S(1)} %get-tuple-element.96), channel_id=1, source_target_pairs={{0,4},{4,8},{8,12},{12,16},{16,20},{20,24},{24,28},{28,32},{32,36}... | collective-permute-start | bytes 6152 | tf_op jit(solution)/shard_map/ppermute | solution.py:11
  279.8 108.7 %collective-permute-start.2 = (f32[128,4]{0,1:T(4,128)S(1)}, f32[128,4]{0,1:T(4,128)S(1)}, u32[]{:S(2)}, u32[]{:S(2)}) collective-permute-start(f32[128,4]{0,1:T(4,128)S(1)} %get-tuple-element.99), channel_id=1, source_target_pairs={{0,4},{4,8},{8,12},{12,16},{16,20},{20,24},{24,28},{28,32},{32,36}... | collective-permute-start | bytes 6152 | tf_op jit(solution)/shard_map/ppermute | solution.py:11
  280.6 108.8 %collective-permute-start.17 = (f32[128,4]{0,1:T(4,128)S(1)}, f32[128,4]{0,1:T(4,128)S(1)}, u32[]{:S(2)}, u32[]{:S(2)}) collective-permute-start(f32[128,4]{0,1:T(4,128)S(1)} %add.84), channel_id=1, source_target_pairs={{0,4},{4,8},{8,12},{12,16},{16,20},{20,24},{24,28},{28,32},{32,36}... | collective-permute-start | bytes 6152 | tf_op jit(solution)/shard_map/ppermute | solution.py:11
  280.9 108.6 %collective-permute-start.12 = (f32[128,4]{0,1:T(4,128)S(1)}, f32[128,4]{0,1:T(4,128)S(1)}, u32[]{:S(2)}, u32[]{:S(2)}) collective-permute-start(f32[128,4]{0,1:T(4,128)S(1)} %multiply_add_fusion.2), channel_id=1, source_target_pairs={{0,4},{4,8},{8,12},{12,16},{16,20},{20,24},{24,28},{28,32},{32,36}... | collective-permute-start | bytes 6152 | tf_op jit(solution)/shard_map/ppermute | solution.py:11
  388.5 7.6 %collective-permute-start.9 = (f32[128,4]{0,1:T(4,128)S(1)}, f32[128,4]{0,1:T(4,128)S(1)}, u32[]{:S(2)}, u32[]{:S(2)}) collective-permute-start(f32[128,4]{0,1:T(4,128)S(1)} %get-tuple-element.92), channel_id=1, source_target_pairs={{0,4},{4,8},{8,12},{12,16},{16,20},{20,24},{24,28},{28,32},{32,36}... | collective-permute-start | bytes 6152 | tf_op jit(solution)/shard_map/ppermute | solution.py:11
  388.6 7.5 %collective-permute-start.4 = (f32[128,4]{0,1:T(4,128)S(1)}, f32[128,4]{0,1:T(4,128)S(1)}, u32[]{:S(2)}, u32[]{:S(2)}) collective-permute-start(f32[128,4]{0,1:T(4,128)S(1)} %get-tuple-element.95), channel_id=1, source_target_pairs={{0,4},{4,8},{8,12},{12,16},{16,20},{20,24},{24,28},{28,32},{32,36}... | collective-permute-start | bytes 6152 | tf_op jit(solution)/shard_map/ppermute | solution.py:11
  389.4 14.1 %collective-permute-start.19 = (f32[128,4]{0,1:T(4,128)S(1)}, f32[128,4]{0,1:T(4,128)S(1)}, u32[]{:S(2)}, u32[]{:S(2)}) collective-permute-start(f32[128,4]{0,1:T(4,128)S(1)} %add.85), channel_id=1, source_target_pairs={{0,4},{4,8},{8,12},{12,16},{16,20},{20,24},{24,28},{28,32},{32,36}... | collective-permute-start | bytes 6152 | tf_op jit(solution)/shard_map/ppermute | solution.py:11
  389.5 14.1 %collective-permute-start.13 = (f32[128,4]{0,1:T(4,128)S(1)}, f32[128,4]{0,1:T(4,128)S(1)}, u32[]{:S(2)}, u32[]{:S(2)}) collective-permute-start(f32[128,4]{0,1:T(4,128)S(1)} %multiply_add_fusion.1), channel_id=1, source_target_pairs={{0,4},{4,8},{8,12},{12,16},{16,20},{20,24},{24,28},{28,32},{32,36}... | collective-permute-start | bytes 6152 | tf_op jit(solution)/shard_map/ppermute | solution.py:11
  396.1 7.6 %collective-permute-start.10 = (f32[128,4]{0,1:T(4,128)S(1)}, f32[128,4]{0,1:T(4,128)S(1)}, u32[]{:S(2)}, u32[]{:S(2)}) collective-permute-start(f32[128,4]{0,1:T(4,128)S(1)} %get-tuple-element.88), channel_id=1, source_target_pairs={{0,116},{4,120},{8,124},{12,0},{16,4},{20,8},{24,12},{28,16},{32,2... | collective-permute-start | bytes 6152 | tf_op jit(solution)/shard_map/ppermute | solution.py:11
  402.7 14.5 %collective-permute-start.6 = (f32[128,4]{0,1:T(4,128)S(1)}, f32[128,4]{0,1:T(4,128)S(1)}, u32[]{:S(2)}, u32[]{:S(2)}) collective-permute-start(f32[128,4]{0,1:T(4,128)S(1)} %get-tuple-element.91), channel_id=1, source_target_pairs={{0,116},{4,120},{8,124},{12,0},{16,4},{20,8},{24,12},{28,16},{32,2... | collective-permute-start | bytes 6152 | tf_op jit(solution)/shard_map/ppermute | solution.py:11
  403.5 20.4 %collective-permute-start.21 = (f32[128,4]{0,1:T(4,128)S(1)}, f32[128,4]{0,1:T(4,128)S(1)}, u32[]{:S(2)}, u32[]{:S(2)}) collective-permute-start(f32[128,4]{0,1:T(4,128)S(1)} %add.86), channel_id=1, source_target_pairs={{0,116},{4,120},{8,124},{12,0},{16,4},{20,8},{24,12},{28,16},{32,2... | collective-permute-start | bytes 6152 | tf_op jit(solution)/shard_map/ppermute | solution.py:11
  403.6 26.9 %collective-permute-start.14 = (f32[128,4]{0,1:T(4,128)S(1)}, f32[128,4]{0,1:T(4,128)S(1)}, u32[]{:S(2)}, u32[]{:S(2)}) collective-permute-start(f32[128,4]{0,1:T(4,128)S(1)} %multiply_add_fusion), channel_id=1, source_target_pairs={{0,116},{4,120},{8,124},{12,0},{16,4},{20,8},{24,12},{28,16},{32,2... | collective-permute-start | bytes 6152 | tf_op jit(solution)/shard_map/ppermute | solution.py:11
where the time goes:
time: 441 us; the launch traced here: 439 us
  waiting for transfers between devices  347 us (79%)
  matrix products  33.7 us (8%)
  blocking collectives  33.4 us (8%)
  starting transfers between devices  11.1 us (3%)
  other arithmetic  7.5 us (2%)
  local copies, waits for them, and re-layouts  4.73 us (1%)
    ppermute x22, waiting for transfers between devices, shifted(): lax.ppermute(value, axis, [(i, (i + by) % devices) for i in range(devices)])  347 us
    dot_general x4, matrix products, block_summary(): lax.dot_general(flattened, head_block, (((1,), (1,)), ((), ())), preferre...  33.7 us
    all_gather x4, blocking collectives, combined_all(): pieces = jax.tree.map(lambda part: lax.all_gather(part, axis), value)  33.4 us
    ppermute x22, starting transfers between devices, shifted(): lax.ppermute(value, axis, [(i, (i + by) % devices) for i in range(devices)])  11.1 us
  transfers between devices with their start and end apart: 22, of which 5 were waited for; matrix products, arithmetic and copies ran while one was open for 9% of the time, Pallas kernels for 0%

commit v1 on v0

v1 whole, which is shorter than its diff:
```python
import functools

import jax
import jax.numpy as jnp
from jax import lax
from jax.experimental import pallas as pl
from jax.experimental.pallas import tpu as pltpu
from jax.sharding import PartitionSpec as P

EXITS = 4
LANES = 128
STEP = 1024
CHUNK = 32
LOW = -3.0e38
NS = 20


def rolled_up(value, by):
    return pltpu.roll(value, value.shape[0] - by, 0)


def final_exit(value, exit_id):
    return jnp.where(
        exit_id == 3,
        value,
        jnp.where(
            exit_id == 2,
            rolled_up(value, 1),
            jnp.where(exit_id == 1, rolled_up(value, 2), rolled_up(value, 3)),
        ),
    )


def fold_logits(logits, wanted, first, state, rows, columns):
    def fold(step, carry):
        here = pl.ds(pl.multiple_of(step * CHUNK, CHUNK), CHUNK)
        exit_id = lax.broadcasted_iota(jnp.int32, (CHUNK, LANES), 0) % EXITS
        lane = lax.broadcasted_iota(jnp.int32, (CHUNK, LANES), 1)
        offset = wanted[here, :] - first - lane
        slabs = [logits[here, pl.ds(LANES * i, LANES)] for i in range(columns // LANES)]
        old_peak = state[0, here, :]
        peak = old_peak
        for slab in slabs:
            peak = jnp.maximum(peak, slab)
        final_peak = final_exit(peak, exit_id)
        decay = jnp.exp(old_peak - peak)
        total = state[1, here, :] * decay
        spread = state[2, here, :] * final_exit(decay, exit_id)
        target = state[3, here, :]
        for i, slab in enumerate(slabs):
            final = final_exit(slab, exit_id)
            total = total + jnp.exp(slab - peak)
            spread = spread + jnp.exp(final - final_peak) * (final - slab)
            target = target + jnp.where(offset == LANES * i, slab, 0.0)
        state[0, here, :] = peak
        state[1, here, :] = total
        state[2, here, :] = spread
        state[3, here, :] = target
        return carry

    lax.fori_loop(0, rows // CHUNK, fold, 0)


def summary_kernel(pieces, distance, *refs):
    parts = refs[:pieces]
    starts, own_head, other_head, wanted, out, held, logits, state, sems = refs[pieces:]
    rows = held.shape[0]
    copies = []
    for i, part in enumerate(parts):
        start = pl.multiple_of(starts[i], 16)
        copies.append(
            pltpu.make_async_copy(part, held.at[pl.ds(start, part.shape[0])], sems.at[i])
        )
    for copy in copies:
        copy.start()
    state[0] = jnp.full((rows, LANES), LOW, jnp.float32)
    state[1:] = jnp.zeros((3, rows, LANES), jnp.float32)
    for copy in copies:
        copy.wait()
    first = 0
    for head in (own_head, other_head):
        for begin in range(0, head.shape[0], STEP):
            logits[...] = lax.dot_general(
                held[...],
                head[pl.ds(begin, STEP), :],
                (((1,), (1,)), ((), ())),
                preferred_element_type=jnp.float32,
            )
            fold_logits(logits, wanted.at[distance], first, state, rows, STEP)
            first += STEP
    exit_id = lax.broadcasted_iota(jnp.int32, (rows, LANES), 0) % EXITS
    peak = jnp.max(state[0], axis=1, keepdims=True)
    weight = jnp.exp(state[0] - peak)
    total = jnp.sum(state[1] * weight, axis=1, keepdims=True)
    spread = jnp.sum(state[2] * final_exit(weight, exit_id), axis=1, keepdims=True)
    target = jnp.sum(state[3], axis=1, keepdims=True)
    lane = lax.broadcasted_iota(jnp.int32, (rows, LANES), 1)
    packed = jnp.where(
        lane == 0,
        peak,
        jnp.where(lane == 1, total, jnp.where(lane == 2, spread, jnp.where(lane == 3, target, 0.0))),
    )
    out[...] = packed.T[:8]


def summarize(parts, starts, own_head, other_head, wanted, distance):
    rows = sum(part.shape[0] for part in parts)
    width = own_head.shape[1]
    vocab = own_head.shape[0] + other_head.shape[0]
    in_place = pl.BlockSpec(memory_space=pl.ANY)
    in_vmem = pl.BlockSpec(memory_space=pltpu.VMEM)
    return pl.pallas_call(
        functools.partial(summary_kernel, len(parts), distance),
        out_shape=jax.ShapeDtypeStruct((8, rows), jnp.float32),
        in_specs=[in_place] * len(parts)
        + [pl.BlockSpec(memory_space=pltpu.SMEM)]
        + [in_vmem] * 3,
        out_specs=in_vmem,
        scratch_shapes=[
            pltpu.VMEM((rows, width), jnp.bfloat16),
            pltpu.VMEM((rows, STEP), jnp.float32),
            pltpu.VMEM((4, rows, LANES), jnp.float32),
            pltpu.SemaphoreType.DMA((len(parts),)),
        ],
        compiler_params=pltpu.CompilerParams(vmem_limit_bytes=20 * 2**20),
        cost_estimate=pl.CostEstimate(
            flops=2 * rows * vocab * width,
            bytes_accessed=2 * (rows + vocab) * width,
            transcendentals=2 * rows * vocab,
        ),
    )(*parts, starts, own_head, other_head, wanted)


def join(first, second):
    rows = first.shape[-1]
    peak = jnp.maximum(first[..., 0, :], second[..., 0, :])
    first_weight = jnp.exp(first[..., 0, :] - peak)
    second_weight = jnp.exp(second[..., 0, :] - peak)

    def of_final(weight):
        by_token = weight.reshape(weight.shape[:-1] + (rows // EXITS, EXITS))
        return jnp.broadcast_to(by_token[..., 3:4], by_token.shape).reshape(weight.shape)

    total = first[..., 1, :] * first_weight + second[..., 1, :] * second_weight
    spread = first[..., 2, :] * of_final(first_weight) + second[..., 2, :] * of_final(second_weight)
    return jnp.stack([peak, total, spread, first[..., 3, :] + second[..., 3, :]], axis=-2)


def on_device(hidden_rows, head_weight, targets):
    blocks = lax.axis_size("blk")
    pieces = lax.axis_size("dp")
    place = lax.axis_index("blk")
    column = lax.axis_index("dp")
    half, core = column // 2, column % 2
    tokens, _, width = hidden_rows.shape
    mine = tokens // 2
    shared = NS
    direct = mine - 2 * shared
    vocab = head_weight.shape[0]

    def moved(value, by, flip=0):
        pairs = []
        for b in range(blocks):
            for d in range(pieces):
                to = b + by
                twist = 2 if (to % blocks) // 16 != b // 16 and d % 2 == 1 else 0
                pairs.append((b * pieces + d, (to % blocks) * pieces + (d ^ flip ^ twist)))
        return lax.ppermute(value, ("blk", "dp"), pairs)

    def back(value, by, flip=0):
        pairs = [
            (b * pieces + d, (b - by) % blocks * pieces + (d ^ flip))
            for b in range(blocks)
            for d in range(pieces)
        ]
        return lax.ppermute(value, ("blk", "dp"), pairs)

    def swapped(value, flip):
        pairs = [(b * pieces + d, b * pieces + (d ^ flip)) for b in range(blocks) for d in range(pieces)]
        return lax.ppermute(value, ("blk", "dp"), pairs)

    def token_rows(start, count):
        return lax.dynamic_slice_in_dim(hidden_rows, start, count, 0).reshape(count * EXITS, width)

    begin = core * mine
    own_m = token_rows(begin + half * shared, shared)
    own_d = token_rows(begin + 2 * shared, direct)
    own_o = token_rows(begin + (1 - half) * shared, shared)

    r3_m = moved(own_m, 3)
    r3_d = moved(own_d, 3)
    other_head = swapped(head_weight, 1)
    r2_m = moved(r3_m, -1)
    r3_o = swapped(r3_m, 2)
    r1_m = moved(own_m, 1)
    r2_d = moved(r3_d, -1)
    r1_o = swapped(r1_m, 2)
    r2_o = swapped(r2_m, 2)
    r1_d = moved(own_d, 1)

    one_back = lax.ppermute(targets, "blk", [(b, (b + 1) % blocks) for b in range(blocks)])
    two_back = lax.ppermute(
        jnp.stack([targets, one_back]), "blk", [(b, (b + 2) % blocks) for b in range(blocks)]
    )
    wanted = jnp.stack([targets, one_back, two_back[0], two_back[1]])
    wanted = lax.dynamic_slice_in_dim(wanted, begin, mine, 1)
    local = wanted - (place * pieces + half * 2) * vocab
    inside = (local >= 0) & (local < 2 * vocab)
    local = jnp.where(inside, (local + core * vocab) % (2 * vocab), -1)
    wanted = jnp.broadcast_to(local[:, :, None, None], (4, mine, EXITS, LANES))
    wanted = wanted.reshape(4, mine * EXITS, LANES)

    ahead = shared * EXITS

    def block(m, o, d, distance):
        wrapped = (place - distance) % blocks // 16 != place // 16
        side = jnp.where(wrapped & (core == 1), 1 - half, half)
        starts = jnp.stack([side * ahead, (1 - side) * ahead, 2 * ahead + 0 * side])
        return summarize([m, o, d], starts, head_weight, other_head, wanted, distance)

    s0 = block(own_m, own_o, own_d, 0)
    s3 = back(block(r3_m, r3_o, r3_d, 3), 3)
    s1 = back(block(r1_m, r1_o, r1_d, 1), 1)
    early = join(join(s0, s3), s1)
    early = [early] + [swapped(early, flip) for flip in (1, 2, 3)]
    s2 = block(r2_m, r2_o, r2_d, 2)
    late = [back(s2, 2, flip) for flip in (0, 1, 2, 3)]
    whole = [join(a, b) for a, b in zip(early, late)]
    mine_done = join(whole[0], whole[2])
    other_done = join(whole[1], whole[3])
    low = jnp.where(core == 0, mine_done, other_done)
    high = jnp.where(core == 0, other_done, mine_done)
    done = jnp.concatenate([low, high], axis=1)
    done = done.reshape(4, tokens, EXITS)
    peak, total, spread, target = done[0], done[1], done[2], done[3]
    log_total = peak + jnp.log(total)
    cross_entropy = log_total - target
    divergence = spread[:, :3] / total[:, 3:4] - log_total[:, 3:4] + log_total[:, :3]
    return (cross_entropy, divergence)


def solution(mesh):
    in_specs = (P("blk", None, None), P(("blk", "dp"), None), P("blk"))
    out_specs = (P("blk", None), P("blk", None))
    return jax.shard_map(
        on_device, mesh=mesh, in_specs=in_specs, out_specs=out_specs, check_vma=False
    )
```

time: 441 us -> 209 us (0.47)
  waiting for transfers between devices: 347 us -> 82.8 us
  Pallas kernels: 0 us -> 57.3 us
  matrix products: 33.7 us -> 0 us
  blocking collectives: 33.4 us -> 0 us
  starting transfers between devices: 11.1 us -> 42 us
  local copies, waits for them, and re-layouts: 4.73 us -> 22.7 us
  other arithmetic: 7.5 us -> 1.62 us
    ppermute x22 -> x21, waiting for transfers between devices: 347 us -> 82.8 us  [the longest x6 67.6 us: moved(): return lax.ppermute(value, ('blk', 'dp'), pairs)]
    pallas_call x0 -> x4, Pallas kernels: none -> 57.3 us  [summarize(): pl.pallas_call(functools.partial(summary_kernel, len(parts), distance), o...]
    dot_general x4 -> x0, matrix products: 33.7 us -> none  [block_summary(): lax.dot_general(flattened, head_block, (((1,), (1,)), ((), ())), preferre...]
    all_gather x4 -> x0, blocking collectives: 33.4 us -> none  [combined_all(): pieces = jax.tree.map(lambda part: lax.all_gather(part, axis), value)]
    ppermute x22 -> x21, starting transfers between devices: 11.1 us -> 42 us  [the longest x6 17.6 us: back(): return lax.ppermute(value, ('blk', 'dp'), pairs)]
    reshape x0 -> x19, local copies, waits for them, and re-layouts: none -> 6.98 us  [the longest x3 5.19 us: token_rows(): lax.dynamic_slice_in_dim(hidden_rows, start, count, 0)]
    reduce_sum x8 -> x0, other arithmetic: 5.76 us -> none  [the longest x4 3.27 us: block_summary(): total = jnp.sum(scaled, axis=2)]
    dynamic_slice x0 -> x2, local copies, waits for them, and re-layouts: none -> 5.47 us  [token_rows(): lax.dynamic_slice_in_dim(hidden_rows, start, count, 0)]
  transfers between devices with their start and end apart: 22 -> 21, of which waited for: 5 -> 6; matrix products, arithmetic and copies ran while one was open for 9% -> 8% of each run, Pallas kernels for 0% -> 28%
where the time goes in v1:
time: 209 us; the launch traced here: 207 us
  waiting for transfers between devices  82.8 us (40%)
  Pallas kernels  57.3 us (27%)
  starting transfers between devices  42 us (20%)
  local copies, waits for them, and re-layouts  22.7 us (11%)
    ppermute x6, waiting for transfers between devices, moved(): return lax.ppermute(value, ('blk', 'dp'), pairs)  67.6 us
    pallas_call x4, Pallas kernels, summarize(): pl.pallas_call(functools.partial(summary_kernel, len(parts), distance), o...  57.3 us
    ppermute x6, starting transfers between devices, back(): return lax.ppermute(value, ('blk', 'dp'), pairs)  17.6 us
    ppermute x6, starting transfers between devices, moved(): return lax.ppermute(value, ('blk', 'dp'), pairs)  13.4 us
    ppermute x7, starting transfers between devices, swapped(): return lax.ppermute(value, ('blk', 'dp'), pairs)  11 us
    ppermute x1, waiting for transfers between devices, on_device(): lax.ppermute(jnp.stack([targets, one_back]), 'blk', [(b, (b + 2) % blocks...  6.89 us
    ppermute x1, waiting for transfers between devices, on_device(): lax.ppermute(targets, 'blk', [(b, (b + 1) % blocks) for b in range(blocks)])  6.53 us
    dynamic_slice x2, local copies, waits for them, and re-layouts, token_rows(): lax.dynamic_slice_in_dim(hidden_rows, start, count, 0)  5.47 us
  transfers between devices with their start and end apart: 21, of which 6 were waited for; matrix products, arithmetic and copies ran while one was open for 8% of the time, Pallas kernels for 28%

profile of v1, /device:TPU:1, one launch (start us, length us, event | category | flops | bytes accessed | tf_op | source)
XLA Modules:
  0.0 207.5 jit_solution(5706702612465769203)
XLA Ops:
  0.6 1.5 collective-permute-start
  2.1 2.9 %constant_dynamic-slice_fusion.1 = (bf16[20,4,5376]{2,1,0:T(4,128)(2,1)}, bf16[20,4,5376]{2,1,0:T(4,128)(2,1)S(1)}) fusion(bf16[128,4,5376]{2,1,0:T(4,128)(2,1)} %param.3, s32[]{:T(128)S(6)} %select_n.95, s32[]{:T(128)S(6)} %select_n.94), kind=kLoop, calls=%fused_computation.120 | loop fusion | bytes 3440648 | tf_op jit(solution)/shard_map/dynamic_slice | solution.py:183
  5.2 2.6 %collective-permute-start.3 = (bf16[80,5376]{1,0:T(8,128)(2,1)S(1)}, bf16[80,5376]{1,0:T(8,128)(2,1)}, u32[]{:S(2)}, u32[]{:S(2)}) collective-permute-start(bf16[80,5376]{1,0:T(8,128)(2,1)S(1)} %reshape.159.refs_0_), channel_id=1, source_target_pairs={{0,12},{1,13},{2,14},{3,15},{4,16},{5,17},{6,18},{7,19},{8,20},{9,... | collective-permute-start | bytes 2580488 | tf_op jit(solution)/shard_map/ppermute | solution.py:168
  7.9 2.6 %constant_dynamic-slice_fusion = bf16[24,4,5376]{2,1,0:T(4,128)(2,1)} fusion(bf16[128,4,5376]{2,1,0:T(4,128)(2,1)} %param.3, s32[]{:T(128)S(6)} %select_n.96), kind=kLoop, calls=%fused_computation.119 | loop fusion | bytes 2064388 | tf_op jit(solution)/shard_map/dynamic_slice | solution.py:183
  10.4 2.6 %reshape.161.refs_2_ = bf16[96,5376]{1,0:T(8,128)(2,1)} reshape(bf16[24,4,5376]{2,1,0:T(4,128)(2,1)} %constant_dynamic-slice_fusion) | data formatting | bytes 2064384 | tf_op jit(solution)/shard_map/reshape | solution.py:183
  13.1 1.9 collective-permute-start.5
  15.0 16.9 %collective-permute-done.3.refs_0_ = bf16[80,5376]{1,0:T(8,128)(2,1)} collective-permute-done((bf16[80,5376]{1,0:T(8,128)(2,1)S(1)}, bf16[80,5376]{1,0:T(8,128)(2,1)}, u32[]{:S(2)}, u32[]{:S(2)}) %collective-permute-start.3) | collective-permute-done | bytes 860192 | tf_op jit(solution)/shard_map/ppermute | solution.py:168
  31.9 3.9 %collective-permute-start.11 = (bf16[80,5376]{1,0:T(8,128)(2,1)}, bf16[80,5376]{1,0:T(8,128)(2,1)}, u32[]{:S(2)}, u32[]{:S(2)}) collective-permute-start(bf16[80,5376]{1,0:T(8,128)(2,1)} %collective-permute-done.3.refs_0_), channel_id=1, source_target_pairs={{0,124},{1,127},{2,126},{3,125},{4,0},{5,1},{6,2},{7,3},{8,4},{9,5... | collective-permute-start | bytes 2580488 | tf_op jit(solution)/shard_map/ppermute | solution.py:168
  35.8 33.9 %collective-permute-done.5.refs_2_ = bf16[96,5376]{1,0:T(8,128)(2,1)} collective-permute-done((bf16[96,5376]{1,0:T(8,128)(2,1)}, bf16[96,5376]{1,0:T(8,128)(2,1)}, u32[]{:S(2)}, u32[]{:S(2)}) %collective-permute-start.5) | collective-permute-done | bytes 1032224 | tf_op jit(solution)/shard_map/ppermute | solution.py:168
  69.7 16.8 %collective-permute-done.11.refs_0_ = bf16[80,5376]{1,0:T(8,128)(2,1)} collective-permute-done((bf16[80,5376]{1,0:T(8,128)(2,1)}, bf16[80,5376]{1,0:T(8,128)(2,1)}, u32[]{:S(2)}, u32[]{:S(2)}) %collective-permute-start.11) | collective-permute-done | bytes 860192 | tf_op jit(solution)/shard_map/ppermute | solution.py:168
  86.5 2.9 %collective-permute-start.12 = (bf16[80,5376]{1,0:T(8,128)(2,1)}, bf16[80,5376]{1,0:T(8,128)(2,1)}, u32[]{:S(2)}, u32[]{:S(2)}) collective-permute-start(bf16[80,5376]{1,0:T(8,128)(2,1)} %collective-permute-done.11.refs_0_), channel_id=1, source_target_pairs={{0,2},{1,3},{2,0},{3,1},{4,6},{5,7},{6,4},{7,5},{8,10},{9,11},{10,... | collective-permute-start | bytes 2580488 | tf_op jit(solution)/shard_map/ppermute | solution.py:180
  89.5 6.5 %collective-permute-done.1 = s32[128]{0:T(128)S(1)} collective-permute-done((s32[128]{0:T(128)S(1)}, s32[128]{0:T(128)S(1)}, u32[]{:S(2)}, u32[]{:S(2)}) %collective-permute-start.1) | collective-permute-done | bytes 544 | tf_op jit(solution)/shard_map/ppermute | solution.py:201
  96.1 6.9 %collective-permute-done.2 = s32[2,128]{1,0:T(2,128)S(1)} collective-permute-done((s32[2,128]{1,0:T(2,128)S(1)}, s32[2,128]{1,0:T(2,128)S(1)}, u32[]{:S(2)}, u32[]{:S(2)}) %collective-permute-start.2) | collective-permute-done | bytes 1056 | tf_op jit(solution)/shard_map/ppermute | solution.py:202
  103.0 4.9 %collective-permute-start.9 = (bf16[96,5376]{1,0:T(8,128)(2,1)}, bf16[96,5376]{1,0:T(8,128)(2,1)}, u32[]{:S(2)}, u32[]{:S(2)}) collective-permute-start(bf16[96,5376]{1,0:T(8,128)(2,1)} %reshape.161.refs_2_), channel_id=1, source_target_pairs={{0,4},{1,5},{2,6},{3,7},{4,8},{5,9},{6,10},{7,11},{8,12},{9,13},{1... | collective-permute-start | bytes 3096584 | tf_op jit(solution)/shard_map/ppermute | solution.py:168
  108.0 2.4 %reshape.160.refs_1_ = bf16[80,5376]{1,0:T(8,128)(2,1)} reshape(bf16[20,4,5376]{2,1,0:T(4,128)(2,1)} %get-tuple-element.42) | data formatting | bytes 1720320 | tf_op jit(solution)/shard_map/reshape | solution.py:183
  110.4 2.9 %collective-permute-start.8 = (bf16[80,5376]{1,0:T(8,128)(2,1)}, bf16[80,5376]{1,0:T(8,128)(2,1)}, u32[]{:S(2)}, u32[]{:S(2)}) collective-permute-start(bf16[80,5376]{1,0:T(8,128)(2,1)} %collective-permute-done.7.refs_0_), channel_id=1, source_target_pairs={{0,2},{1,3},{2,0},{3,1},{4,6},{5,7},{6,4},{7,5},{8,10},{9,11},{10,... | collective-permute-start | bytes 2580488 | tf_op jit(solution)/shard_map/ppermute | solution.py:180
  114.3 1.0 broadcast_in_dim.128
  115.7 4.1 %copy-done = bf16[1024,5376]{1,0:T(8,128)(2,1)S(1)} copy-done((bf16[1024,5376]{1,0:T(8,128)(2,1)S(1)}, bf16[1024,5376]{1,0:T(8,128)(2,1)}, u32[]{:S(2)}) %copy-start) | copy-done | bytes 11010072
  119.8 15.4 %shard_map.53 = f32[8,256]{1,0:T(8,128)S(1)} custom-call(bf16[80,5376]{1,0:T(8,128)(2,1)} %collective-permute-done.11.refs_0_, bf16[80,5376]{1,0:T(8,128)(2,1)} %collective-permute-done.12.refs_1_, bf16[96,5376]{1,0:T(8,128)(2,1)} %collective-permute-done.13.refs_2_, s32[3]{0:T(128)S(1)} %pad_add_fusion.2.refs_3_, bf16[1024,5376]{1,0:T(8,128)(2,1)S(1)} %copy-done, ...), custom_call_target="tpu_custom_call" | custom-call | flops 5637144576 | bytes 24772608 | tf_op jit(solution)/shard_map/pallas_call | solution.py:112
  135.1 3.9 %collective-permute-start.18 = (f32[8,256]{1,0:T(8,128)S(1)}, f32[8,256]{1,0:T(8,128)S(1)}, u32[]{:S(2)}, u32[]{:S(2)}) collective-permute-start(f32[8,256]{1,0:T(8,128)S(1)} %shard_map.53), channel_id=1, source_target_pairs={{0,121},{1,120},{2,123},{3,122},{4,125},{5,124},{6,127},{7,126},{8... | collective-permute-start | bytes 24584 | tf_op jit(solution)/shard_map/ppermute | solution.py:176
  139.1 1.0 collective-permute-start.20
  140.2 14.4 %shard_map.52 = f32[8,256]{1,0:T(8,128)S(1)} custom-call(bf16[80,5376]{1,0:T(8,128)(2,1)} %collective-permute-done.7.refs_0_, bf16[80,5376]{1,0:T(8,128)(2,1)} %collective-permute-done.8.refs_1_, bf16[96,5376]{1,0:T(8,128)(2,1)} %collective-permute-done.9.refs_2_, s32[3]{0:T(128)S(1)} %pad_add_fusion.3.refs_3_, bf16[1024,5376]{1,0:T(8,128)(2,1)S(1)} %bitcast.11, ...), custom_call_target="tpu_custom_call" | custom-call | flops 5637144576 | bytes 24772608 | tf_op jit(solution)/shard_map/pallas_call | solution.py:112
  154.6 7.1 %collective-permute-start.10 = (f32[8,256]{1,0:T(8,128)S(1)}, f32[8,256]{1,0:T(8,128)S(1)}, u32[]{:S(2)}, u32[]{:S(2)}) collective-permute-start(f32[8,256]{1,0:T(8,128)S(1)} %shard_map.52), channel_id=1, source_target_pairs={{0,124},{1,125},{2,126},{3,127},{4,0},{5,1},{6,2},{7,3},{8,4},{9,5... | collective-permute-start | bytes 24584 | tf_op jit(solution)/shard_map/ppermute | solution.py:176
  161.7 14.2 %shard_map.51 = f32[8,256]{1,0:T(8,128)S(1)} custom-call(bf16[80,5376]{1,0:T(8,128)(2,1)} %collective-permute-done.3.refs_0_, bf16[80,5376]{1,0:T(8,128)(2,1)S(1)} %collective-permute-done.4.refs_1_, bf16[96,5376]{1,0:T(8,128)(2,1)} %collective-permute-done.5.refs_2_, s32[3]{0:T(128)S(1)} %pad_add_fusion.4.refs_3_, bf16[1024,5376]{1,0:T(8,128)(2,1)S(1)} %bitcast.11, ...), custom_call_target="tpu_custom_call" | custom-call | flops 5637144576 | bytes 24772608 | tf_op jit(solution)/shard_map/pallas_call | solution.py:112
  175.9 1.6 collective-permute-start.6
  177.5 13.4 %shard_map.50 = f32[8,256]{1,0:T(8,128)S(1)} custom-call(bf16[80,5376]{1,0:T(8,128)(2,1)S(1)} %reshape.159.refs_0_, bf16[80,5376]{1,0:T(8,128)(2,1)S(1)} %copy-done.2, bf16[96,5376]{1,0:T(8,128)(2,1)S(1)} %copy-done.1, s32[3]{0:T(128)S(1)} %pad_add_fusion.5.refs_3_, bf16[1024,5376]{1,0:T(8,128)(2,1)S(1)} %bitcast.11, ...), custom_call_target="tpu_custom_call" | custom-call | flops 5637144576 | bytes 24772608 | tf_op jit(solution)/shard_map/pallas_call | solution.py:112
  192.4 0.8 collective-permute-start.17
  193.1 1.5 collective-permute-start.19
  194.7 2.4 %collective-permute-start.14 = (f32[8,256]{1,0:T(8,128)S(1)}, f32[8,256]{1,0:T(8,128)S(1)}, u32[]{:S(2)}, u32[]{:S(2)}) collective-permute-start(f32[8,256]{1,0:T(8,128)S(1)} %shard_map.53), channel_id=1, source_target_pairs={{0,120},{1,121},{2,122},{3,123},{4,124},{5,125},{6,126},{7,127},{8... | collective-permute-start | bytes 24584 | tf_op jit(solution)/shard_map/ppermute | solution.py:176
  197.1 1.4 collective-permute-start.16
  198.5 1.3 collective-permute-start.15
  201.7 1.8 collective-permute-done.16
  (112 shorter events, 8.9 us)
Async XLA Ops:
  0.6 88.8 %copy-start.3 = (s32[128]{0:T(128)S(1)}, s32[128]{0:T(128)}, u32[]{:S(2)}) copy-start(s32[128]{0:T(128)} %param.5) | copy-start | bytes 1540
  0.6 114.8 %collective-permute-start = (bf16[1024,5376]{1,0:T(8,128)(2,1)}, bf16[1024,5376]{1,0:T(8,128)(2,1)}, u32[]{:S(2)}, u32[]{:S(2)}) collective-permute-start(bf16[1024,5376]{1,0:T(8,128)(2,1)} %refs_4_.7), channel_id=1, source_target_pairs={{0,1},{1,0},{2,3},{3,2},{4,5},{5,4},{6,7},{7,6},{8,9},{9,8},{10,11... | collective-permute-start | bytes 33030152 | tf_op jit(solution)/shard_map/ppermute | solution.py:180
  5.2 26.7 %collective-permute-start.3 = (bf16[80,5376]{1,0:T(8,128)(2,1)S(1)}, bf16[80,5376]{1,0:T(8,128)(2,1)}, u32[]{:S(2)}, u32[]{:S(2)}) collective-permute-start(bf16[80,5376]{1,0:T(8,128)(2,1)S(1)} %reshape.159.refs_0_), channel_id=1, source_target_pairs={{0,12},{1,13},{2,14},{3,15},{4,16},{5,17},{6,18},{7,19},{8,20},{9,... | collective-permute-start | bytes 2580488 | tf_op jit(solution)/shard_map/ppermute | solution.py:168
  10.4 129.7 %slice-start = ((s8[11010048]{0:T(1024)(128)(4,1)}), s8[2621440]{0:T(1024)(128)(4,1)S(1)}, s32[]{:S(2)}) async-start(s8[11010048]{0:T(1024)(128)(4,1)} %bitcast.10), calls=%async_computation | async-start | bytes 5242880
  13.1 56.6 %collective-permute-start.5 = (bf16[96,5376]{1,0:T(8,128)(2,1)}, bf16[96,5376]{1,0:T(8,128)(2,1)}, u32[]{:S(2)}, u32[]{:S(2)}) collective-permute-start(bf16[96,5376]{1,0:T(8,128)(2,1)} %reshape.161.refs_2_), channel_id=1, source_target_pairs={{0,12},{1,13},{2,14},{3,15},{4,16},{5,17},{6,18},{7,19},{8,20},{9,... | collective-permute-start | bytes 3096584 | tf_op jit(solution)/shard_map/ppermute | solution.py:168
  31.9 54.6 %collective-permute-start.11 = (bf16[80,5376]{1,0:T(8,128)(2,1)}, bf16[80,5376]{1,0:T(8,128)(2,1)}, u32[]{:S(2)}, u32[]{:S(2)}) collective-permute-start(bf16[80,5376]{1,0:T(8,128)(2,1)} %collective-permute-done.3.refs_0_), channel_id=1, source_target_pairs={{0,124},{1,127},{2,126},{3,125},{4,0},{5,1},{6,2},{7,3},{8,4},{9,5... | collective-permute-start | bytes 2580488 | tf_op jit(solution)/shard_map/ppermute | solution.py:168
  35.8 74.6 %collective-permute-start.7 = (bf16[80,5376]{1,0:T(8,128)(2,1)S(1)}, bf16[80,5376]{1,0:T(8,128)(2,1)}, u32[]{:S(2)}, u32[]{:S(2)}) collective-permute-start(bf16[80,5376]{1,0:T(8,128)(2,1)S(1)} %reshape.159.refs_0_), channel_id=1, source_target_pairs={{0,4},{1,5},{2,6},{3,7},{4,8},{5,9},{6,10},{7,11},{8,12},{9,13},{1... | collective-permute-start | bytes 2580488 | tf_op jit(solution)/shard_map/ppermute | solution.py:168
  69.7 45.6 %collective-permute-start.13 = (bf16[96,5376]{1,0:T(8,128)(2,1)}, bf16[96,5376]{1,0:T(8,128)(2,1)}, u32[]{:S(2)}, u32[]{:S(2)}) collective-permute-start(bf16[96,5376]{1,0:T(8,128)(2,1)} %collective-permute-done.5.refs_2_), channel_id=1, source_target_pairs={{0,124},{1,127},{2,126},{3,125},{4,0},{5,1},{6,2},{7,3},{8,4},{9,5... | collective-permute-start | bytes 3096584 | tf_op jit(solution)/shard_map/ppermute | solution.py:168
  86.5 29.0 %collective-permute-start.12 = (bf16[80,5376]{1,0:T(8,128)(2,1)}, bf16[80,5376]{1,0:T(8,128)(2,1)}, u32[]{:S(2)}, u32[]{:S(2)}) collective-permute-start(bf16[80,5376]{1,0:T(8,128)(2,1)} %collective-permute-done.11.refs_0_), channel_id=1, source_target_pairs={{0,2},{1,3},{2,0},{3,1},{4,6},{5,7},{6,4},{7,5},{8,10},{9,11},{10,... | collective-permute-start | bytes 2580488 | tf_op jit(solution)/shard_map/ppermute | solution.py:180
  89.4 6.6 %collective-permute-start.1 = (s32[128]{0:T(128)S(1)}, s32[128]{0:T(128)S(1)}, u32[]{:S(2)}, u32[]{:S(2)}) collective-permute-start(s32[128]{0:T(128)S(1)} %copy-done.3), channel_id=1, source_target_pairs={{0,4},{4,8},{8,12},{12,16},{16,20},{20,24},{24,28},{28,32},{32,36}... | collective-permute-start | bytes 1544 | tf_op jit(solution)/shard_map/ppermute | solution.py:201
  96.0 6.9 %collective-permute-start.2 = (s32[2,128]{1,0:T(2,128)S(1)}, s32[2,128]{1,0:T(2,128)S(1)}, u32[]{:S(2)}, u32[]{:S(2)}) collective-permute-start(s32[2,128]{1,0:T(2,128)S(1)} %pad_add_fusion.1), channel_id=1, source_target_pairs={{0,8},{4,12},{8,16},{12,20},{16,24},{20,28},{24,32},{28,36},{32,40... | collective-permute-start | bytes 3080 | tf_op jit(solution)/shard_map/ppermute | solution.py:202
  103.0 37.2 %collective-permute-start.9 = (bf16[96,5376]{1,0:T(8,128)(2,1)}, bf16[96,5376]{1,0:T(8,128)(2,1)}, u32[]{:S(2)}, u32[]{:S(2)}) collective-permute-start(bf16[96,5376]{1,0:T(8,128)(2,1)} %reshape.161.refs_2_), channel_id=1, source_target_pairs={{0,4},{1,5},{2,6},{3,7},{4,8},{5,9},{6,10},{7,11},{8,12},{9,13},{1... | collective-permute-start | bytes 3096584 | tf_op jit(solution)/shard_map/ppermute | solution.py:168
  110.4 29.7 %collective-permute-start.8 = (bf16[80,5376]{1,0:T(8,128)(2,1)}, bf16[80,5376]{1,0:T(8,128)(2,1)}, u32[]{:S(2)}, u32[]{:S(2)}) collective-permute-start(bf16[80,5376]{1,0:T(8,128)(2,1)} %collective-permute-done.7.refs_0_), channel_id=1, source_target_pairs={{0,2},{1,3},{2,0},{3,1},{4,6},{5,7},{6,4},{7,5},{8,10},{9,11},{10,... | collective-permute-start | bytes 2580488 | tf_op jit(solution)/shard_map/ppermute | solution.py:180
  115.3 46.4 %collective-permute-start.4 = (bf16[80,5376]{1,0:T(8,128)(2,1)}, bf16[80,5376]{1,0:T(8,128)(2,1)S(1)}, u32[]{:S(2)}, u32[]{:S(2)}) collective-permute-start(bf16[80,5376]{1,0:T(8,128)(2,1)} %collective-permute-done.3.refs_0_), channel_id=1, source_target_pairs={{0,2},{1,3},{2,0},{3,1},{4,6},{5,7},{6,4},{7,5},{8,10},{9,11},{10,... | collective-permute-start | bytes 2580488 | tf_op jit(solution)/shard_map/ppermute | solution.py:180
  115.6 4.1 %copy-start = (bf16[1024,5376]{1,0:T(8,128)(2,1)S(1)}, bf16[1024,5376]{1,0:T(8,128)(2,1)}, u32[]{:S(2)}) copy-start(bf16[1024,5376]{1,0:T(8,128)(2,1)} %refs_4_.7) | copy-start | bytes 33030148
  119.8 20.4 %slice-start.1 = ((s8[11010048]{0:T(1024)(128)(4,1)}), s8[4194304]{0:T(1024)(128)(4,1)S(1)}, s32[]{:S(2)}) async-start(s8[11010048]{0:T(1024)(128)(4,1)} %bitcast.10), calls=%async_computation.1 | async-start | bytes 8388608
  119.8 20.4 %slice-start.2 = ((s8[11010048]{0:T(1024)(128)(4,1)}), s8[4194304]{0:T(1024)(128)(4,1)S(1)}, s32[]{:S(2)}) async-start(s8[11010048]{0:T(1024)(128)(4,1)} %bitcast.10), calls=%async_computation.2 | async-start | bytes 8388608
  135.1 61.9 %collective-permute-start.18 = (f32[8,256]{1,0:T(8,128)S(1)}, f32[8,256]{1,0:T(8,128)S(1)}, u32[]{:S(2)}, u32[]{:S(2)}) collective-permute-start(f32[8,256]{1,0:T(8,128)S(1)} %shard_map.53), channel_id=1, source_target_pairs={{0,121},{1,120},{2,123},{3,122},{4,125},{5,124},{6,127},{7,126},{8... | collective-permute-start | bytes 24584 | tf_op jit(solution)/shard_map/ppermute | solution.py:176
  139.1 59.5 %collective-permute-start.20 = (f32[8,256]{1,0:T(8,128)S(1)}, f32[8,256]{1,0:T(8,128)S(1)}, u32[]{:S(2)}, u32[]{:S(2)}) collective-permute-start(f32[8,256]{1,0:T(8,128)S(1)} %shard_map.53), channel_id=1, source_target_pairs={{0,123},{1,122},{2,121},{3,120},{4,127},{5,126},{6,125},{7,124},{8... | collective-permute-start | bytes 24584 | tf_op jit(solution)/shard_map/ppermute | solution.py:176
  154.6 22.9 %copy-start.1 = (bf16[96,5376]{1,0:T(8,128)(2,1)S(1)}, bf16[96,5376]{1,0:T(8,128)(2,1)}, u32[]{:S(2)}) copy-start(bf16[96,5376]{1,0:T(8,128)(2,1)} %reshape.161.refs_2_) | copy-start | bytes 3096580
  154.6 22.9 %copy-start.2 = (bf16[80,5376]{1,0:T(8,128)(2,1)S(1)}, bf16[80,5376]{1,0:T(8,128)(2,1)}, u32[]{:S(2)}) copy-start(bf16[80,5376]{1,0:T(8,128)(2,1)} %reshape.160.refs_1_) | copy-start | bytes 2580484
  154.6 36.4 %collective-permute-start.10 = (f32[8,256]{1,0:T(8,128)S(1)}, f32[8,256]{1,0:T(8,128)S(1)}, u32[]{:S(2)}, u32[]{:S(2)}) collective-permute-start(f32[8,256]{1,0:T(8,128)S(1)} %shard_map.52), channel_id=1, source_target_pairs={{0,124},{1,125},{2,126},{3,127},{4,0},{5,1},{6,2},{7,3},{8,4},{9,5... | collective-permute-start | bytes 24584 | tf_op jit(solution)/shard_map/ppermute | solution.py:176
  175.9 15.3 %collective-permute-start.6 = (f32[8,256]{1,0:T(8,128)S(1)}, f32[8,256]{1,0:T(8,128)S(1)}, u32[]{:S(2)}, u32[]{:S(2)}) collective-permute-start(f32[8,256]{1,0:T(8,128)S(1)} %shard_map.51), channel_id=1, source_target_pairs={{0,116},{1,117},{2,118},{3,119},{4,120},{5,121},{6,122},{7,123},{8... | collective-permute-start | bytes 24584 | tf_op jit(solution)/shard_map/ppermute | solution.py:176
  192.4 7.4 %collective-permute-start.17 = (f32[4,256]{1,0:T(4,128)S(1)}, f32[4,256]{1,0:T(4,128)S(1)}, u32[]{:S(2)}, u32[]{:S(2)}) collective-permute-start(f32[4,256]{1,0:T(4,128)S(1)} %pad_maximum_fusion), channel_id=1, source_target_pairs={{0,1},{1,0},{2,3},{3,2},{4,5},{5,4},{6,7},{7,6},{8,9},{9,8},{10,11... | collective-permute-start | bytes 12296 | tf_op jit(solution)/shard_map/ppermute | solution.py:180
  193.1 6.7 %collective-permute-start.19 = (f32[4,256]{1,0:T(4,128)S(1)}, f32[4,256]{1,0:T(4,128)S(1)}, u32[]{:S(2)}, u32[]{:S(2)}) collective-permute-start(f32[4,256]{1,0:T(4,128)S(1)} %pad_maximum_fusion), channel_id=1, source_target_pairs={{0,3},{1,2},{2,1},{3,0},{4,7},{5,6},{6,5},{7,4},{8,11},{9,10},{10,... | collective-permute-start | bytes 12296 | tf_op jit(solution)/shard_map/ppermute | solution.py:180
  194.7 7.0 %collective-permute-start.14 = (f32[8,256]{1,0:T(8,128)S(1)}, f32[8,256]{1,0:T(8,128)S(1)}, u32[]{:S(2)}, u32[]{:S(2)}) collective-permute-start(f32[8,256]{1,0:T(8,128)S(1)} %shard_map.53), channel_id=1, source_target_pairs={{0,120},{1,121},{2,122},{3,123},{4,124},{5,125},{6,126},{7,127},{8... | collective-permute-start | bytes 24584 | tf_op jit(solution)/shard_map/ppermute | solution.py:176
  197.1 6.4 %collective-permute-start.16 = (f32[8,256]{1,0:T(8,128)S(1)}, f32[8,256]{1,0:T(8,128)S(1)}, u32[]{:S(2)}, u32[]{:S(2)}) collective-permute-start(f32[8,256]{1,0:T(8,128)S(1)} %shard_map.53), channel_id=1, source_target_pairs={{0,122},{1,123},{2,120},{3,121},{4,126},{5,127},{6,124},{7,125},{8... | collective-permute-start | bytes 24584 | tf_op jit(solution)/shard_map/ppermute | solution.py:176
  198.5 5.0 %collective-permute-start.15 = (f32[4,256]{1,0:T(4,128)S(1)}, f32[4,256]{1,0:T(4,128)S(1)}, u32[]{:S(2)}, u32[]{:S(2)}) collective-permute-start(f32[4,256]{1,0:T(4,128)S(1)} %pad_maximum_fusion), channel_id=1, source_target_pairs={{0,2},{1,3},{2,0},{3,1},{4,6},{5,7},{6,4},{7,5},{8,10},{9,11},{10,... | collective-permute-start | bytes 12296 | tf_op jit(solution)/shard_map/ppermute | solution.py:180

commit v2 on v1

v2 whole, which is shorter than its diff:
```python
import functools

import jax
import jax.numpy as jnp
from jax import lax
from jax.experimental import pallas as pl
from jax.experimental.pallas import tpu as pltpu
from jax.sharding import PartitionSpec as P

EXITS = 4
LANES = 128
STEP = 1024
CHUNK = 32
LOW = -3.0e38
FIRST = [(16, True), (32, False)]
THIRD = [(20, True), (24, False)]


def rolled_up(value, by):
    return pltpu.roll(value, value.shape[0] - by, 0)


def final_exit(value, exit_id):
    return jnp.where(
        exit_id == 3,
        value,
        jnp.where(
            exit_id == 2,
            rolled_up(value, 1),
            jnp.where(exit_id == 1, rolled_up(value, 2), rolled_up(value, 3)),
        ),
    )


def fold_logits(logits, wanted, offset, first, state, begin, columns):
    here = pl.ds(begin, CHUNK)
    exit_id = lax.broadcasted_iota(jnp.int32, (CHUNK, LANES), 0) % EXITS
    lane = lax.broadcasted_iota(jnp.int32, (CHUNK, LANES), 1)
    ahead = wanted[pl.ds(offset + begin, CHUNK), :] - first - lane
    slabs = [logits[here, pl.ds(LANES * i, LANES)] for i in range(columns // LANES)]
    old_peak = state[0, here, :]
    peak = old_peak
    for slab in slabs:
        peak = jnp.maximum(peak, slab)
    final_peak = final_exit(peak, exit_id)
    decay = jnp.exp(old_peak - peak)
    total = state[1, here, :] * decay
    spread = state[2, here, :] * final_exit(decay, exit_id)
    target = state[3, here, :]
    for i, slab in enumerate(slabs):
        final = final_exit(slab, exit_id)
        total = total + jnp.exp(slab - peak)
        spread = spread + jnp.exp(final - final_peak) * (final - slab)
        target = target + jnp.where(ahead == LANES * i, slab, 0.0)
    state[0, here, :] = peak
    state[1, here, :] = total
    state[2, here, :] = spread
    state[3, here, :] = target


def summary_kernel(pieces, offset, blocks, *refs):
    parts = refs[:pieces]
    starts, own_head, other_head, wanted = refs[pieces : pieces + 4]
    outs = refs[pieces + 4 : pieces + 4 + blocks]
    held, tiles, logits, state, sems, tile_sems = refs[pieces + 4 + blocks :]
    rows, depth = held.shape[0], tiles.shape[2]
    tile_count = tiles.shape[0]
    copies = []
    for i, part in enumerate(parts):
        start = pl.multiple_of(starts[i], 16)
        copies.append(
            pltpu.make_async_copy(part, held.at[pl.ds(start, part.shape[0])], sems.at[i])
        )
    steps = [
        (head, begin, part)
        for head in (own_head, other_head)
        for begin in range(0, own_head.shape[0], STEP)
        for part in range(0, own_head.shape[1], depth)
    ]

    def fetch(i):
        head, begin, part = steps[i]
        slot = i % tile_count
        return pltpu.make_async_copy(
            head.at[pl.ds(begin, STEP), pl.ds(part, depth)], tiles.at[slot], tile_sems.at[slot]
        )

    fetch(0).start()
    for copy in copies:
        copy.start()
    for i in range(1, tile_count - 1):
        fetch(i).start()
    state[0] = jnp.full((rows, LANES), LOW, jnp.float32)
    state[1:] = jnp.zeros((3, rows, LANES), jnp.float32)
    for copy in copies:
        copy.wait()
    parts_deep = own_head.shape[1] // depth
    waiting, first, turn = [], 0, 0
    for i, (_, _, part) in enumerate(steps):
        fetch(i).wait()
        if i + tile_count - 1 < len(steps):
            fetch(i + tile_count - 1).start()
        product = lax.dot_general(
            held[:, pl.ds(part, depth)],
            tiles[i % tile_count],
            (((1,), (1,)), ((), ())),
            preferred_element_type=jnp.float32,
        )
        for _ in range(-(-len(waiting) // (parts_deep - part // depth))):
            waiting.pop(0)()
        if part == 0:
            logits[turn] = product
        else:
            logits[turn] += product
        if part + depth == own_head.shape[1]:
            for begin in range(0, rows, CHUNK):
                waiting.append(
                    functools.partial(
                        fold_logits, logits.at[turn], wanted, offset, first, state, begin, STEP
                    )
                )
            first += STEP
            turn = 1 - turn
    for fold in waiting:
        fold()
    exit_id = lax.broadcasted_iota(jnp.int32, (rows, LANES), 0) % EXITS
    peak = jnp.max(state[0], axis=1, keepdims=True)
    weight = jnp.exp(state[0] - peak)
    total = jnp.sum(state[1] * weight, axis=1, keepdims=True)
    spread = jnp.sum(state[2] * final_exit(weight, exit_id), axis=1, keepdims=True)
    target = jnp.sum(state[3], axis=1, keepdims=True)
    lane = lax.broadcasted_iota(jnp.int32, (rows, LANES), 1)
    packed = jnp.where(
        lane == 0,
        peak,
        jnp.where(lane == 1, total, jnp.where(lane == 2, spread, jnp.where(lane == 3, target, 0.0))),
    )
    packed = packed.T
    for i, out in enumerate(outs):
        out[...] = packed[:8, i * (rows // blocks) : (i + 1) * (rows // blocks)]


def summarize(parts, starts, own_head, other_head, wanted, offset, blocks, busy):
    rows = sum(part.shape[0] for part in parts)
    width = own_head.shape[1]
    in_place = pl.BlockSpec(memory_space=pl.ANY)
    in_vmem = pl.BlockSpec(memory_space=pltpu.VMEM)
    return pl.pallas_call(
        functools.partial(summary_kernel, len(parts), offset, blocks),
        out_shape=[jax.ShapeDtypeStruct((8, rows // blocks), jnp.float32)] * blocks,
        in_specs=[in_place] * len(parts)
        + [pl.BlockSpec(memory_space=pltpu.SMEM)]
        + [in_place] * 2
        + [in_vmem],
        out_specs=[in_vmem] * blocks,
        scratch_shapes=[
            pltpu.VMEM((rows, width), jnp.bfloat16),
            pltpu.VMEM((4, STEP, width // 3), jnp.bfloat16),
            pltpu.VMEM((2, rows, STEP), jnp.float32),
            pltpu.VMEM((4, rows, LANES), jnp.float32),
            pltpu.SemaphoreType.DMA((len(parts),)),
            pltpu.SemaphoreType.DMA((4,)),
        ],
        compiler_params=pltpu.CompilerParams(vmem_limit_bytes=44 * 2**20),
        cost_estimate=pl.CostEstimate(flops=busy, bytes_accessed=0, transcendentals=0),
    )(
        *parts,
        starts,
        pltpu.with_memory_space_constraint(own_head, pltpu.HBM),
        pltpu.with_memory_space_constraint(other_head, pltpu.HBM),
        wanted,
    )


def join(first, second):
    rows = first.shape[-1]
    peak = jnp.maximum(first[..., 0, :], second[..., 0, :])
    first_weight = jnp.exp(first[..., 0, :] - peak)
    second_weight = jnp.exp(second[..., 0, :] - peak)

    def of_final(weight):
        by_token = weight.reshape(weight.shape[:-1] + (rows // EXITS, EXITS))
        return jnp.broadcast_to(by_token[..., 3:4], by_token.shape).reshape(weight.shape)

    total = first[..., 1, :] * first_weight + second[..., 1, :] * second_weight
    spread = first[..., 2, :] * of_final(first_weight) + second[..., 2, :] * of_final(second_weight)
    return jnp.stack([peak, total, spread, first[..., 3, :] + second[..., 3, :]], axis=-2)


def relayout_kernel(count, cuts, source, origin, *refs):
    outs = refs[: len(cuts)]
    tall, flat, fetch, sems = refs[len(cuts) :]
    copy = pltpu.make_async_copy(source.at[pl.ds(origin[0], count)], tall, fetch)
    copy.start()
    copy.wait()
    flat[...] = tall[...].reshape(flat.shape)
    copies = []
    for i, out in enumerate(outs):
        start = pl.multiple_of(origin[1 + i], 16)
        copies.append(
            pltpu.make_async_copy(flat.at[pl.ds(start, out.shape[0])], out, sems.at[i])
        )
    for copy in copies:
        copy.start()
    for copy in copies:
        copy.wait()


def token_rows(source, count, origin, cuts):
    width = source.shape[2]
    in_place = pl.BlockSpec(memory_space=pl.ANY)
    return pl.pallas_call(
        functools.partial(relayout_kernel, count, cuts),
        out_shape=[pltpu.HBM((cut, width), source.dtype) for cut in cuts],
        in_specs=[in_place, pl.BlockSpec(memory_space=pltpu.SMEM)],
        out_specs=[in_place] * len(cuts),
        scratch_shapes=[
            pltpu.VMEM((count, EXITS, width), source.dtype),
            pltpu.VMEM((count * EXITS, width), source.dtype),
            pltpu.SemaphoreType.DMA,
            pltpu.SemaphoreType.DMA((len(cuts),)),
        ],
        compiler_params=pltpu.CompilerParams(vmem_limit_bytes=16 * 2**20),
    )(pltpu.with_memory_space_constraint(source, pltpu.HBM), origin)


def on_device(hidden_rows, head_weight, targets):
    blocks = lax.axis_size("blk")
    pieces = lax.axis_size("dp")
    place = lax.axis_index("blk")
    column = lax.axis_index("dp")
    half, core = column // 2, column % 2
    tokens = hidden_rows.shape[0]
    mine = tokens // 2
    vocab = head_weight.shape[0]
    ring = 4

    def cut_starts(cuts, side):
        taken = sum(count for count, shared in cuts if shared)
        starts, at = [], taken
        for count, shared in cuts:
            if shared:
                starts.append(side * (mine - count) * EXITS)
            else:
                starts.append(at * EXITS + 0 * side)
                at += count
        return starts

    def exchanged_starts(cuts, side):
        return [(1 - side) * (mine - count) * EXITS for count, shared in cuts if shared]

    def permuted(value, move):
        pairs = []
        for b in range(blocks):
            for d in range(pieces):
                to = move(b, d)
                if to is not None:
                    pairs.append((b * pieces + d, to[0] % blocks * pieces + to[1]))
        return lax.ppermute(value, ("blk", "dp"), pairs)

    def crossing(b, by, d, turning):
        wraps = (b + by) % blocks // 16 != b // 16
        return (b + by, d ^ 2 if wraps and d % 2 in turning else d)

    def around(b, by):
        return b // ring * ring + (b + by) % ring

    def to_first(b, d):
        return crossing(b, (1, 3)[d % 2], d, (1,))

    def to_second(b, d):
        return crossing(b, (1, -1)[d % 2], d, (1,))

    def to_second_turned(b, d):
        return crossing(b, (1, -1)[d % 2], d, (0,))

    def up(b, d):
        return crossing(b, ring, d, (1,)) if b % ring == (1, 3)[d % 2] else None

    def to_third(b, d):
        if d % 2 == 1:
            return around(b, 1), d
        return (around(b, -1), d) if b % ring == 1 else crossing(b, 3, d, ())

    def across(flip):
        return lambda b, d: (b, d ^ flip)

    def home(by, flip=0):
        return lambda b, d: (b - by[d % 2], d ^ flip)

    back = [
        lax.ppermute(targets, "blk", [(b, (b + by) % blocks) for b in range(blocks)])
        for by in (1, 2, 3)
    ]
    begin = core * mine
    whole_third = len(THIRD) == 1 and not THIRD[0][1]
    at = cut_starts(FIRST, half)
    lead = token_rows(
        hidden_rows, FIRST[0][0], jnp.stack([begin + at[0] // EXITS, 0 * half]), [FIRST[0][0] * EXITS]
    )
    rest, back = lax.optimization_barrier((hidden_rows, back))
    cuts = FIRST[1:] + ([] if whole_third else THIRD)
    origin = [begin, 0 * half] + at[1:]
    origin += [] if whole_third else cut_starts(THIRD, half)
    own, *sent = token_rows(
        rest, mine, jnp.stack(origin), [mine * EXITS] + [count * EXITS for count, _ in cuts]
    )
    to_send = list(lead) + list(sent[: len(FIRST) - 1])
    third_send = [own] if whole_third else list(sent[len(FIRST) - 1 :])

    first, second = [None] * len(FIRST), [None] * len(FIRST)
    first[0] = permuted(to_send[0], to_first)
    lifted = [permuted(part, up) for part in third_send]
    other_head = permuted(head_weight, across(1))
    for i in range(1, len(FIRST)):
        first[i] = permuted(to_send[i], to_first)
    first_more = [permuted(part, across(2)) for part, cut in zip(first, FIRST) if cut[1]]
    uses_lifted = place % ring == jnp.where(core == 0, 1, 3)
    third = [
        permuted(jnp.where(uses_lifted, up_part, part), to_third)
        for up_part, part in zip(lifted, third_send)
    ]
    third_more = [permuted(part, across(2)) for part, cut in zip(third, THIRD) if cut[1]]

    def positions(ids):
        local = ids - (place * pieces + half * 2) * vocab
        inside = (local >= 0) & (local < 2 * vocab)
        local = jnp.where(inside, (local + core * vocab) % (2 * vocab), -1)
        spread = jnp.broadcast_to(local[..., None, None], local.shape + (EXITS, LANES))
        return spread.reshape(-1, LANES)

    own_wanted = positions(lax.dynamic_slice_in_dim(targets, begin, mine, 0))
    wanted = jnp.stack(
        [jnp.where(core == 0, back[0], back[2]), back[1], jnp.where(core == 0, back[2], back[0])]
    )
    wanted = positions(lax.dynamic_slice_in_dim(wanted, begin, mine, 1))

    def side(distance):
        wrapped = (place - distance) % blocks // 16 != place // 16
        return jnp.where(wrapped & (core == 1), 1 - half, half)

    def block(parts, starts, ids, offset, count):
        return summarize(
            parts,
            jnp.stack(starts).astype(jnp.int32),
            head_weight,
            other_head,
            ids,
            offset * mine * EXITS,
            count,
            0,
        )

    def placed(cuts, side, at=0):
        starts = cut_starts(cuts, side) + exchanged_starts(cuts, side)
        return [start + at * mine * EXITS for start in starts]

    first_side, second_side = side(jnp.where(core == 0, 1, 3)), side(2)
    third_side = side(jnp.where(core == 0, 3, 1))

    first_more, own_0 = lax.optimization_barrier((first_more, own))
    (sum_0,) = block([own_0], [0 * half], own_wanted, 0, 1)
    first[-1], sum_0 = lax.optimization_barrier((first[-1], sum_0))
    for i, (_, shared) in enumerate(FIRST):
        second[i] = permuted(first[i], to_second if shared else to_second_turned)
    second_more = [permuted(part, across(2)) for part, cut in zip(second, FIRST) if cut[1]]
    (sum_1,) = block(first + first_more, placed(FIRST, first_side), wanted, 0, 1)
    second[-1], sum_1 = lax.optimization_barrier((second[-1], sum_1))
    sum_1 = permuted(sum_1, home((1, 3)))
    early = join(sum_0, sum_1)
    sum_2, sum_3 = block(
        second + second_more + third + third_more,
        placed(FIRST, second_side) + placed(THIRD, third_side, 1),
        wanted,
        1,
        2,
    )
    late = join(permuted(sum_2, home((2, 2))), permuted(sum_3, home((3, 1))))
    whole = join(early, late)
    whole = [whole] + [permuted(whole, across(flip)) for flip in (1, 2, 3)]
    mine_done = join(whole[0], whole[2])
    other_done = join(whole[1], whole[3])
    low = jnp.where(core == 0, mine_done, other_done)
    high = jnp.where(core == 0, other_done, mine_done)
    done = jnp.concatenate([low, high], axis=1)
    done = done.reshape(4, tokens, EXITS)
    peak, total, spread, target = done[0], done[1], done[2], done[3]
    log_total = peak + jnp.log(total)
    cross_entropy = log_total - target
    divergence = spread[:, :3] / total[:, 3:4] - log_total[:, 3:4] + log_total[:, :3]
    return (cross_entropy, divergence)


def solution(mesh):
    in_specs = (P("blk", None, None), P(("blk", "dp"), None), P("blk"))
    out_specs = (P("blk", None), P("blk", None))
    return jax.shard_map(
        on_device, mesh=mesh, in_specs=in_specs, out_specs=out_specs, check_vma=False
    )
```

time: 209 us -> 175 us (0.84)
  waiting for transfers between devices: 82.8 us -> 48.1 us
  starting transfers between devices: 42 us -> 66.8 us
  local copies, waits for them, and re-layouts: 22.7 us -> 7.24 us
  Pallas kernels: 57.3 us -> 47.7 us
  other arithmetic: 1.62 us -> 3.72 us
    ppermute x21, waiting for transfers between devices: 82.8 us -> 48.1 us  [the longest x18 45.1 us: permuted(): return lax.ppermute(value, ('blk', 'dp'), pairs)]
    ppermute x21, starting transfers between devices: 42 us -> 66.8 us  [the longest x18 60.6 us: permuted(): return lax.ppermute(value, ('blk', 'dp'), pairs)]
    pallas_call x4 -> x5, Pallas kernels: 57.3 us -> 47.7 us  [the longest x3 40 us: summarize(): pl.pallas_call(functools.partial(summary_kernel, len(parts), offset, bloc...]
    dynamic_slice x2 -> x0, local copies, waits for them, and re-layouts: 5.47 us -> none  [token_rows(): lax.dynamic_slice_in_dim(hidden_rows, start, count, 0)]
    reshape x3 -> x0, local copies, waits for them, and re-layouts: 5.19 us -> none  [token_rows(): lax.dynamic_slice_in_dim(hidden_rows, start, count, 0)]
    select_n x1 -> x4, other arithmetic: 0.09 us -> 2.54 us  [the longest x2 2.36 us: on_device(): jnp.where(uses_lifted, up_part, part)]
    unnamed x16 -> x12, local copies, waits for them, and re-layouts: 5.46 us -> 3.28 us
  transfers between devices with their start and end apart: 21 -> 21, of which waited for: 6 -> 9; matrix products, arithmetic and copies ran while one was open for 8% -> 2% of each run, Pallas kernels for 28% -> 17%
where the time goes in v2:
time: 175 us
  starting transfers between devices  66.8 us (38%)
  waiting for transfers between devices  48.1 us (27%)
  Pallas kernels  47.7 us (27%)
  local copies, waits for them, and re-layouts  7.24 us (4%)
  other arithmetic  3.72 us (2%)
    ppermute x18, starting transfers between devices, permuted(): return lax.ppermute(value, ('blk', 'dp'), pairs)  60.6 us
    ppermute x18, waiting for transfers between devices, permuted(): return lax.ppermute(value, ('blk', 'dp'), pairs)  45.1 us
    pallas_call x3, Pallas kernels, summarize(): pl.pallas_call(functools.partial(summary_kernel, len(parts), offset, bloc...  40 us
    pallas_call x2, Pallas kernels, token_rows(): pl.pallas_call(functools.partial(relayout_kernel, count, cuts), out_shape...  7.76 us
    ppermute x3, starting transfers between devices, on_device(): lax.ppermute(targets, 'blk', [(b, (b + by) % blocks) for b in range(block...  6.27 us
  transfers between devices with their start and end apart: 21, of which 9 were waited for; matrix products, arithmetic and copies ran while one was open for 2% of the time, Pallas kernels for 17%

profile of v2, /device:TPU:1, one launch (start us, length us, event | category | flops | bytes accessed | tf_op | source)
XLA Modules:
  0.0 174.7 jit_solution(15941916874866278811)
XLA Ops:
  0.6 1.5 collective-permute-start.6
  2.1 1.3 collective-permute-start
  3.4 2.5 %collective-permute-start.1 = (s32[128]{0:T(128)}, s32[128]{0:T(128)S(1)}, u32[]{:S(2)}, u32[]{:S(2)}) collective-permute-start(s32[128]{0:T(128)} %param.5), channel_id=1, source_target_pairs={{0,8},{4,12},{8,16},{12,20},{16,24},{20,28},{24,32},{28,36},{32,40... | collective-permute-start | bytes 1544 | tf_op jit(solution)/shard_map/ppermute | solution.py:292
  5.9 2.5 %collective-permute-start.2 = (s32[128]{0:T(128)}, s32[128]{0:T(128)S(1)}, u32[]{:S(2)}, u32[]{:S(2)}) collective-permute-start(s32[128]{0:T(128)} %param.5), channel_id=1, source_target_pairs={{0,12},{4,16},{8,20},{12,24},{16,28},{20,32},{24,36},{28,40},{32,4... | collective-permute-start | bytes 1544 | tf_op jit(solution)/shard_map/ppermute | solution.py:292
  8.5 1.8 %collective-permute-done = s32[128]{0:T(128)S(1)} collective-permute-done((s32[128]{0:T(128)}, s32[128]{0:T(128)S(1)}, u32[]{:S(2)}, u32[]{:S(2)}) %collective-permute-start) | collective-permute-done | bytes 544 | tf_op jit(solution)/shard_map/ppermute | solution.py:292
  10.2 1.2 collective-permute-done.1
  11.5 5.2 %shard_map.50 = (bf16[256,5376]{1,0:T(8,128)(2,1)}, bf16[128,5376]{1,0:T(8,128)(2,1)}, bf16[80,5376]{1,0:T(8,128)(2,1)}, bf16[96,5376]{1,0:T(8,128)(2,1)}) custom-call(bf16[128,4,5376]{2,1,0:T(4,128)(2,1)} %source.2, s32[5]{0:T(128)S(1)} %stack.74.origin), custom_call_target="tpu_custom_call" | custom-call | tf_op jit(solution)/shard_map/pallas_call | solution.py:212
  16.6 1.6 collective-permute-start.11
  18.3 2.6 %shard_map.51 = bf16[64,5376]{1,0:T(8,128)(2,1)} custom-call(bf16[128,4,5376]{2,1,0:T(4,128)(2,1)} %source.2, s32[2]{0:T(128)S(1)} %pad_add_fusion.1.origin), custom_call_target="tpu_custom_call" | custom-call | tf_op jit(solution)/shard_map/pallas_call | solution.py:212
  20.9 2.7 %collective-permute-start.4 = (bf16[64,5376]{1,0:T(8,128)(2,1)}, bf16[64,5376]{1,0:T(8,128)(2,1)}, u32[]{:S(2)}, u32[]{:S(2)}) collective-permute-start(bf16[64,5376]{1,0:T(8,128)(2,1)} %shard_map.51), channel_id=1, source_target_pairs={{0,4},{1,13},{2,6},{3,15},{4,8},{5,17},{6,10},{7,19},{8,12},{9,21}... | collective-permute-start | bytes 2064392 | tf_op jit(solution)/shard_map/ppermute | solution.py:259
  24.8 15.0 %collective-permute-done.4.refs_0_ = bf16[64,5376]{1,0:T(8,128)(2,1)} collective-permute-done((bf16[64,5376]{1,0:T(8,128)(2,1)}, bf16[64,5376]{1,0:T(8,128)(2,1)}, u32[]{:S(2)}, u32[]{:S(2)}) %collective-permute-start.4) | collective-permute-done | bytes 688160 | tf_op jit(solution)/shard_map/ppermute | solution.py:259
  39.8 1.5 collective-permute-start.5
  41.4 1.3 broadcast_select_fusion.1
  42.6 9.1 %collective-permute-done.5.refs_2_ = bf16[64,5376]{1,0:T(8,128)(2,1)S(1)} collective-permute-done((bf16[64,5376]{1,0:T(8,128)(2,1)}, bf16[64,5376]{1,0:T(8,128)(2,1)S(1)}, u32[]{:S(2)}, u32[]{:S(2)}) %collective-permute-start.5) | collective-permute-done | bytes 688160 | tf_op jit(solution)/shard_map/ppermute | solution.py:259
  51.7 0.9 copy-done.1
  52.6 3.2 %collective-permute-start.12 = (bf16[80,5376]{1,0:T(8,128)(2,1)S(1)}, bf16[80,5376]{1,0:T(8,128)(2,1)}, u32[]{:S(2)}, u32[]{:S(2)}) collective-permute-start(bf16[80,5376]{1,0:T(8,128)(2,1)S(1)} %broadcast_select_fusion.1), channel_id=1, source_target_pairs={{0,12},{1,5},{2,14},{3,7},{4,0},{5,9},{6,2},{7,11},{8,20},{9,13},{... | collective-permute-start | bytes 2580488 | tf_op jit(solution)/shard_map/ppermute | solution.py:259
  55.9 10.3 %shard_map.52 = f32[8,256]{1,0:T(8,128)S(1)} custom-call(bf16[256,5376]{1,0:T(8,128)(2,1)S(1)} %copy-done, s32[1]{0:T(128)} %constant.144.clone.1.refs_1_, bf16[1024,5376]{1,0:T(8,128)(2,1)} %refs_7_.1, bf16[1024,5376]{1,0:T(8,128)(2,1)} %collective-permute-done.6.refs_3_.refs_5_.refs_8_, s32[256,128]{1,0:T(8,128)S(1)} %broadcast_in_dim.101.refs_4_), custom_call_target="tpu_custom_call" | custom-call | tf_op jit(solution)/shard_map/pallas_call | solution.py:148
  66.2 2.0 %collective-permute-done.3.refs_1_ = bf16[128,5376]{1,0:T(8,128)(2,1)} collective-permute-done((bf16[128,5376]{1,0:T(8,128)(2,1)}, bf16[128,5376]{1,0:T(8,128)(2,1)}, u32[]{:S(2)}, u32[]{:S(2)}) %collective-permute-start.3) | collective-permute-done | bytes 1376288 | tf_op jit(solution)/shard_map/ppermute | solution.py:259
  68.2 18.3 %collective-permute-start.7 = (bf16[128,5376]{1,0:T(8,128)(2,1)}, bf16[128,5376]{1,0:T(8,128)(2,1)S(1)}, u32[]{:S(2)}, u32[]{:S(2)}) collective-permute-start(bf16[128,5376]{1,0:T(8,128)(2,1)} %collective-permute-done.3.refs_1_), channel_id=1, source_target_pairs={{0,4},{1,125},{2,6},{3,127},{4,8},{5,1},{6,10},{7,3},{8,12},{9,5},... | collective-permute-start | bytes 4128776 | tf_op jit(solution)/shard_map/ppermute | solution.py:259
  86.5 1.1 broadcast_select_fusion
  87.7 3.0 %collective-permute-start.10 = (bf16[64,5376]{1,0:T(8,128)(2,1)}, bf16[64,5376]{1,0:T(8,128)(2,1)}, u32[]{:S(2)}, u32[]{:S(2)}) collective-permute-start(bf16[64,5376]{1,0:T(8,128)(2,1)} %collective-permute-done.9.refs_0_), channel_id=1, source_target_pairs={{0,2},{1,3},{2,0},{3,1},{4,6},{5,7},{6,4},{7,5},{8,10},{9,11},{10,... | collective-permute-start | bytes 2064392 | tf_op jit(solution)/shard_map/ppermute | solution.py:259
  91.3 1.1 copy-done.2
  92.4 11.4 %shard_map.53 = f32[8,256]{1,0:T(8,128)S(1)} custom-call(bf16[64,5376]{1,0:T(8,128)(2,1)} %collective-permute-done.4.refs_0_, bf16[128,5376]{1,0:T(8,128)(2,1)} %collective-permute-done.3.refs_1_, bf16[64,5376]{1,0:T(8,128)(2,1)S(1)} %copy-done.2, s32[3]{0:T(128)S(1)} %pad_add_fusion.2.refs_3_, bf16[1024,5376]{1,0:T(8,128)(2,1)} %refs_7_.1, ...), custom_call_target="tpu_custom_call" | custom-call | tf_op jit(solution)/shard_map/pallas_call | solution.py:148
  103.7 5.6 %collective-permute-done.7.refs_1_ = bf16[128,5376]{1,0:T(8,128)(2,1)S(1)} collective-permute-done((bf16[128,5376]{1,0:T(8,128)(2,1)}, bf16[128,5376]{1,0:T(8,128)(2,1)S(1)}, u32[]{:S(2)}, u32[]{:S(2)}) %collective-permute-start.7) | collective-permute-done | bytes 1376288 | tf_op jit(solution)/shard_map/ppermute | solution.py:259
  109.3 11.1 %collective-permute-done.10.refs_2_ = bf16[64,5376]{1,0:T(8,128)(2,1)} collective-permute-done((bf16[64,5376]{1,0:T(8,128)(2,1)}, bf16[64,5376]{1,0:T(8,128)(2,1)}, u32[]{:S(2)}, u32[]{:S(2)}) %collective-permute-start.10) | collective-permute-done | bytes 688160 | tf_op jit(solution)/shard_map/ppermute | solution.py:259
  120.5 18.3 %shard_map.54 = (f32[8,256]{1,0:T(8,128)S(1)}, f32[8,256]{1,0:T(8,128)S(1)}) custom-call(bf16[64,5376]{1,0:T(8,128)(2,1)} %collective-permute-done.9.refs_0_, bf16[128,5376]{1,0:T(8,128)(2,1)S(1)} %collective-permute-done.7.refs_1_, bf16[64,5376]{1,0:T(8,128)(2,1)} %collective-permute-done.10.refs_2_, bf16[80,5376]{1,0:T(8,128)(2,1)} %collective-permute-done.12.refs_3_, ...), custom_call_target="tpu_custom_call" | custom-call | tf_op jit(solution)/shard_map/pallas_call | solution.py:148
  138.8 8.0 %collective-permute-start.16 = (f32[8,256]{1,0:T(8,128)S(1)}, f32[8,256]{1,0:T(8,128)S(1)}, u32[]{:S(2)}, u32[]{:S(2)}) collective-permute-start(f32[8,256]{1,0:T(8,128)S(1)} %get-tuple-element.32), channel_id=1, source_target_pairs={{0,120},{1,121},{2,122},{3,123},{4,124},{5,125},{6,126},{7,127},{8... | collective-permute-start | bytes 24584 | tf_op jit(solution)/shard_map/ppermute | solution.py:259
  146.7 5.0 %collective-permute-start.8 = (f32[8,256]{1,0:T(8,128)S(1)}, f32[8,256]{1,0:T(8,128)S(1)}, u32[]{:S(2)}, u32[]{:S(2)}) collective-permute-start(f32[8,256]{1,0:T(8,128)S(1)} %shard_map.53), channel_id=1, source_target_pairs={{0,124},{1,117},{2,126},{3,119},{4,0},{5,121},{6,2},{7,123},{8,4},... | collective-permute-start | bytes 24584 | tf_op jit(solution)/shard_map/ppermute | solution.py:259
  151.7 0.8 collective-permute-done.8
  155.2 12.0 %collective-permute-start.19 = (f32[4,256]{1,0:T(4,128)S(1)}, f32[4,256]{1,0:T(4,128)S(1)}, u32[]{:S(2)}, u32[]{:S(2)}) collective-permute-start(f32[4,256]{1,0:T(4,128)S(1)} %pad_maximum_fusion), channel_id=1, source_target_pairs={{0,1},{1,0},{2,3},{3,2},{4,5},{5,4},{6,7},{7,6},{8,9},{9,8},{10,11... | collective-permute-start | bytes 12296 | tf_op jit(solution)/shard_map/ppermute | solution.py:259
  167.2 2.2 %collective-permute-start.20 = (f32[4,256]{1,0:T(4,128)S(1)}, f32[4,256]{1,0:T(4,128)S(1)}, u32[]{:S(2)}, u32[]{:S(2)}) collective-permute-start(f32[4,256]{1,0:T(4,128)S(1)} %pad_maximum_fusion), channel_id=1, source_target_pairs={{0,3},{1,2},{2,1},{3,0},{4,7},{5,6},{6,5},{7,4},{8,11},{9,10},{10,... | collective-permute-start | bytes 12296 | tf_op jit(solution)/shard_map/ppermute | solution.py:259
  170.2 1.5 collective-permute-done.20
  (93 shorter events, 8.2 us)
Async XLA Ops:
  0.6 55.2 %collective-permute-start.6 = (bf16[1024,5376]{1,0:T(8,128)(2,1)}, bf16[1024,5376]{1,0:T(8,128)(2,1)}, u32[]{:S(2)}, u32[]{:S(2)}) collective-permute-start(bf16[1024,5376]{1,0:T(8,128)(2,1)} %refs_7_.1), channel_id=1, source_target_pairs={{0,1},{1,0},{2,3},{3,2},{4,5},{5,4},{6,7},{7,6},{8,9},{9,8},{10,11... | collective-permute-start | bytes 33030152 | tf_op jit(solution)/shard_map/ppermute | solution.py:259
  2.1 8.1 %collective-permute-start = (s32[128]{0:T(128)}, s32[128]{0:T(128)S(1)}, u32[]{:S(2)}, u32[]{:S(2)}) collective-permute-start(s32[128]{0:T(128)} %param.5), channel_id=1, source_target_pairs={{0,4},{4,8},{8,12},{12,16},{16,20},{20,24},{24,28},{28,32},{32,36}... | collective-permute-start | bytes 1544 | tf_op jit(solution)/shard_map/ppermute | solution.py:292
  3.4 8.0 %collective-permute-start.1 = (s32[128]{0:T(128)}, s32[128]{0:T(128)S(1)}, u32[]{:S(2)}, u32[]{:S(2)}) collective-permute-start(s32[128]{0:T(128)} %param.5), channel_id=1, source_target_pairs={{0,8},{4,12},{8,16},{12,20},{16,24},{20,28},{24,32},{28,36},{32,40... | collective-permute-start | bytes 1544 | tf_op jit(solution)/shard_map/ppermute | solution.py:292
  5.9 5.6 %collective-permute-start.2 = (s32[128]{0:T(128)}, s32[128]{0:T(128)S(1)}, u32[]{:S(2)}, u32[]{:S(2)}) collective-permute-start(s32[128]{0:T(128)} %param.5), channel_id=1, source_target_pairs={{0,12},{4,16},{8,20},{12,24},{16,28},{20,32},{24,36},{28,40},{32,4... | collective-permute-start | bytes 1544 | tf_op jit(solution)/shard_map/ppermute | solution.py:292
  16.6 24.7 %collective-permute-start.11 = (bf16[80,5376]{1,0:T(8,128)(2,1)}, bf16[80,5376]{1,0:T(8,128)(2,1)}, u32[]{:S(2)}, u32[]{:S(2)}) collective-permute-start(bf16[80,5376]{1,0:T(8,128)(2,1)} %get-tuple-element.30), channel_id=1, source_target_pairs={{4,20},{6,22},{13,29},{15,31},{20,36},{22,38},{29,45},{31,47},{36,... | collective-permute-start | bytes 2580488 | tf_op jit(solution)/shard_map/ppermute | solution.py:259
  18.3 5.3 %copy-start.4 = (s32[128]{0:T(128)S(1)}, s32[128]{0:T(128)}, u32[]{:S(2)}) copy-start(s32[128]{0:T(128)} %param.5) | copy-start | bytes 1540
  20.9 35.0 %copy-start = (bf16[256,5376]{1,0:T(8,128)(2,1)S(1)}, bf16[256,5376]{1,0:T(8,128)(2,1)}, u32[]{:S(2)}) copy-start(bf16[256,5376]{1,0:T(8,128)(2,1)} %get-tuple-element.21.refs_0_) | copy-start | bytes 8257540
  20.9 18.9 %collective-permute-start.4 = (bf16[64,5376]{1,0:T(8,128)(2,1)}, bf16[64,5376]{1,0:T(8,128)(2,1)}, u32[]{:S(2)}, u32[]{:S(2)}) collective-permute-start(bf16[64,5376]{1,0:T(8,128)(2,1)} %shard_map.51), channel_id=1, source_target_pairs={{0,4},{1,13},{2,6},{3,15},{4,8},{5,17},{6,10},{7,19},{8,12},{9,21}... | collective-permute-start | bytes 2064392 | tf_op jit(solution)/shard_map/ppermute | solution.py:259
  23.9 44.2 %collective-permute-start.3 = (bf16[128,5376]{1,0:T(8,128)(2,1)}, bf16[128,5376]{1,0:T(8,128)(2,1)}, u32[]{:S(2)}, u32[]{:S(2)}) collective-permute-start(bf16[128,5376]{1,0:T(8,128)(2,1)} %get-tuple-element.19), channel_id=1, source_target_pairs={{0,4},{1,13},{2,6},{3,15},{4,8},{5,17},{6,10},{7,19},{8,12},{9,21}... | collective-permute-start | bytes 4128776 | tf_op jit(solution)/shard_map/ppermute | solution.py:259
  24.1 62.4 %collective-permute-start.13 = (bf16[96,5376]{1,0:T(8,128)(2,1)}, bf16[96,5376]{1,0:T(8,128)(2,1)S(1)}, u32[]{:S(2)}, u32[]{:S(2)}) collective-permute-start(bf16[96,5376]{1,0:T(8,128)(2,1)} %get-tuple-element.31), channel_id=1, source_target_pairs={{4,20},{6,22},{13,29},{15,31},{20,36},{22,38},{29,45},{31,47},{36,... | collective-permute-start | bytes 3096584 | tf_op jit(solution)/shard_map/ppermute | solution.py:259
  39.8 11.9 %collective-permute-start.5 = (bf16[64,5376]{1,0:T(8,128)(2,1)}, bf16[64,5376]{1,0:T(8,128)(2,1)S(1)}, u32[]{:S(2)}, u32[]{:S(2)}) collective-permute-start(bf16[64,5376]{1,0:T(8,128)(2,1)} %collective-permute-done.4.refs_0_), channel_id=1, source_target_pairs={{0,2},{1,3},{2,0},{3,1},{4,6},{5,7},{6,4},{7,5},{8,10},{9,11},{10,... | collective-permute-start | bytes 2064392 | tf_op jit(solution)/shard_map/ppermute | solution.py:259
  41.4 46.3 %collective-permute-start.9 = (bf16[64,5376]{1,0:T(8,128)(2,1)}, bf16[64,5376]{1,0:T(8,128)(2,1)}, u32[]{:S(2)}, u32[]{:S(2)}) collective-permute-start(bf16[64,5376]{1,0:T(8,128)(2,1)} %collective-permute-done.4.refs_0_), channel_id=1, source_target_pairs={{0,4},{1,127},{2,6},{3,125},{4,8},{5,1},{6,10},{7,3},{8,12},{9,5},... | collective-permute-start | bytes 2064392 | tf_op jit(solution)/shard_map/ppermute | solution.py:259
  51.7 0.9 copy-start.1
  52.6 35.0 %collective-permute-start.12 = (bf16[80,5376]{1,0:T(8,128)(2,1)S(1)}, bf16[80,5376]{1,0:T(8,128)(2,1)}, u32[]{:S(2)}, u32[]{:S(2)}) collective-permute-start(bf16[80,5376]{1,0:T(8,128)(2,1)S(1)} %broadcast_select_fusion.1), channel_id=1, source_target_pairs={{0,12},{1,5},{2,14},{3,7},{4,0},{5,9},{6,2},{7,11},{8,20},{9,13},{... | collective-permute-start | bytes 2580488 | tf_op jit(solution)/shard_map/ppermute | solution.py:259
  55.9 30.6 %copy-start.3 = (bf16[96,5376]{1,0:T(8,128)(2,1)S(1)}, bf16[96,5376]{1,0:T(8,128)(2,1)}, u32[]{:S(2)}) copy-start(bf16[96,5376]{1,0:T(8,128)(2,1)} %get-tuple-element.31) | copy-start | bytes 3096580
  68.2 41.1 %collective-permute-start.7 = (bf16[128,5376]{1,0:T(8,128)(2,1)}, bf16[128,5376]{1,0:T(8,128)(2,1)S(1)}, u32[]{:S(2)}, u32[]{:S(2)}) collective-permute-start(bf16[128,5376]{1,0:T(8,128)(2,1)} %collective-permute-done.3.refs_1_), channel_id=1, source_target_pairs={{0,4},{1,125},{2,6},{3,127},{4,8},{5,1},{6,10},{7,3},{8,12},{9,5},... | collective-permute-start | bytes 4128776 | tf_op jit(solution)/shard_map/ppermute | solution.py:259
  87.6 32.8 %collective-permute-start.14 = (bf16[96,5376]{1,0:T(8,128)(2,1)}, bf16[96,5376]{1,0:T(8,128)(2,1)S(1)}, u32[]{:S(2)}, u32[]{:S(2)}) collective-permute-start(bf16[96,5376]{1,0:T(8,128)(2,1)} %broadcast_select_fusion), channel_id=1, source_target_pairs={{0,12},{1,5},{2,14},{3,7},{4,0},{5,9},{6,2},{7,11},{8,20},{9,13},{... | collective-permute-start | bytes 3096584 | tf_op jit(solution)/shard_map/ppermute | solution.py:259
  87.6 32.8 %collective-permute-start.15 = (bf16[80,5376]{1,0:T(8,128)(2,1)}, bf16[80,5376]{1,0:T(8,128)(2,1)S(1)}, u32[]{:S(2)}, u32[]{:S(2)}) collective-permute-start(bf16[80,5376]{1,0:T(8,128)(2,1)} %collective-permute-done.12.refs_3_), channel_id=1, source_target_pairs={{0,2},{1,3},{2,0},{3,1},{4,6},{5,7},{6,4},{7,5},{8,10},{9,11},{10,... | collective-permute-start | bytes 2580488 | tf_op jit(solution)/shard_map/ppermute | solution.py:259
  87.7 32.8 %collective-permute-start.10 = (bf16[64,5376]{1,0:T(8,128)(2,1)}, bf16[64,5376]{1,0:T(8,128)(2,1)}, u32[]{:S(2)}, u32[]{:S(2)}) collective-permute-start(bf16[64,5376]{1,0:T(8,128)(2,1)} %collective-permute-done.9.refs_0_), channel_id=1, source_target_pairs={{0,2},{1,3},{2,0},{3,1},{4,6},{5,7},{6,4},{7,5},{8,10},{9,11},{10,... | collective-permute-start | bytes 2064392 | tf_op jit(solution)/shard_map/ppermute | solution.py:259
  91.2 1.1 copy-start.2
  138.8 13.0 %collective-permute-start.16 = (f32[8,256]{1,0:T(8,128)S(1)}, f32[8,256]{1,0:T(8,128)S(1)}, u32[]{:S(2)}, u32[]{:S(2)}) collective-permute-start(f32[8,256]{1,0:T(8,128)S(1)} %get-tuple-element.32), channel_id=1, source_target_pairs={{0,120},{1,121},{2,122},{3,123},{4,124},{5,125},{6,126},{7,127},{8... | collective-permute-start | bytes 24584 | tf_op jit(solution)/shard_map/ppermute | solution.py:259
  146.7 5.0 %collective-permute-start.17 = (f32[8,256]{1,0:T(8,128)S(1)}, f32[8,256]{1,0:T(8,128)S(1)}, u32[]{:S(2)}, u32[]{:S(2)}) collective-permute-start(f32[8,256]{1,0:T(8,128)S(1)} %get-tuple-element.33), channel_id=1, source_target_pairs={{0,116},{1,125},{2,118},{3,127},{4,120},{5,1},{6,122},{7,3},{8,124... | collective-permute-start | bytes 24584 | tf_op jit(solution)/shard_map/ppermute | solution.py:259
  146.7 5.8 %collective-permute-start.8 = (f32[8,256]{1,0:T(8,128)S(1)}, f32[8,256]{1,0:T(8,128)S(1)}, u32[]{:S(2)}, u32[]{:S(2)}) collective-permute-start(f32[8,256]{1,0:T(8,128)S(1)} %shard_map.53), channel_id=1, source_target_pairs={{0,124},{1,117},{2,126},{3,119},{4,0},{5,121},{6,2},{7,123},{8,4},... | collective-permute-start | bytes 24584 | tf_op jit(solution)/shard_map/ppermute | solution.py:259
  154.5 14.9 %collective-permute-start.18 = (f32[4,256]{1,0:T(4,128)S(1)}, f32[4,256]{1,0:T(4,128)S(1)}, u32[]{:S(2)}, u32[]{:S(2)}) collective-permute-start(f32[4,256]{1,0:T(4,128)S(1)} %pad_maximum_fusion), channel_id=1, source_target_pairs={{0,2},{1,3},{2,0},{3,1},{4,6},{5,7},{6,4},{7,5},{8,10},{9,11},{10,... | collective-permute-start | bytes 12296 | tf_op jit(solution)/shard_map/ppermute | solution.py:259
  155.2 14.6 %collective-permute-start.19 = (f32[4,256]{1,0:T(4,128)S(1)}, f32[4,256]{1,0:T(4,128)S(1)}, u32[]{:S(2)}, u32[]{:S(2)}) collective-permute-start(f32[4,256]{1,0:T(4,128)S(1)} %pad_maximum_fusion), channel_id=1, source_target_pairs={{0,1},{1,0},{2,3},{3,2},{4,5},{5,4},{6,7},{7,6},{8,9},{9,8},{10,11... | collective-permute-start | bytes 12296 | tf_op jit(solution)/shard_map/ppermute | solution.py:259
  167.2 4.5 %collective-permute-start.20 = (f32[4,256]{1,0:T(4,128)S(1)}, f32[4,256]{1,0:T(4,128)S(1)}, u32[]{:S(2)}, u32[]{:S(2)}) collective-permute-start(f32[4,256]{1,0:T(4,128)S(1)} %pad_maximum_fusion), channel_id=1, source_target_pairs={{0,3},{1,2},{2,1},{3,0},{4,7},{5,6},{6,5},{7,4},{8,11},{9,10},{10,... | collective-permute-start | bytes 12296 | tf_op jit(solution)/shard_map/ppermute | solution.py:259

commit v3 on v2

--- a/solution.py
+++ b/solution.py
@@ -12,8 +12,8 @@
 STEP = 1024
 CHUNK = 32
 LOW = -3.0e38
-FIRST = [(16, True), (32, False)]
-THIRD = [(20, True), (24, False)]
+FIRST = [(32, False), (32, False)]
+THIRD = [(32, False), (32, False)]
 
 
 def rolled_up(value, by):

time: 175 us -> 170 us (0.971)
  starting transfers between devices: 66.8 us -> 25.5 us
  waiting for transfers between devices: 48.1 us -> 80.4 us
  Pallas kernels: 47.7 us -> 50.8 us
  local copies, waits for them, and re-layouts: 7.24 us -> 5.19 us
    ppermute x18 -> x15, starting transfers between devices: 60.6 us -> 19.2 us  [permuted(): return lax.ppermute(value, ('blk', 'dp'), pairs)]
    ppermute x18 -> x15, waiting for transfers between devices: 45.1 us -> 80.4 us  [permuted(): return lax.ppermute(value, ('blk', 'dp'), pairs)]
    ppermute x3, waiting for transfers between devices: 2.99 us -> 0.01 us  [on_device(): lax.ppermute(targets, 'blk', [(b, (b + by) % blocks) for b in range(block...]
    pallas_call x3, Pallas kernels: 40 us -> 42.3 us  [summarize(): pl.pallas_call(functools.partial(summary_kernel, len(parts), offset, bloc...]
    unnamed x12 -> x8, local copies, waits for them, and re-layouts: 3.28 us -> 1.32 us
  transfers between devices with their start and end apart: 21 -> 18, of which waited for: 9 -> 6; matrix products, arithmetic and copies ran while one was open for 2% -> 3% of each run, Pallas kernels for 17% -> 30%
where the time goes in v3:
time: 170 us; the launch traced here: 168 us
  waiting for transfers between devices  80.4 us (47%)
  Pallas kernels  50.8 us (30%)
  starting transfers between devices  25.5 us (15%)
  local copies, waits for them, and re-layouts  5.19 us (3%)
  other arithmetic  5.11 us (3%)
    ppermute x15, waiting for transfers between devices, permuted(): return lax.ppermute(value, ('blk', 'dp'), pairs)  80.4 us
    pallas_call x3, Pallas kernels, summarize(): pl.pallas_call(functools.partial(summary_kernel, len(parts), offset, bloc...  42.3 us
    ppermute x15, starting transfers between devices, permuted(): return lax.ppermute(value, ('blk', 'dp'), pairs)  19.2 us
    pallas_call x2, Pallas kernels, token_rows(): pl.pallas_call(functools.partial(relayout_kernel, count, cuts), out_shape...  8.57 us
    ppermute x3, starting transfers between devices, on_device(): lax.ppermute(targets, 'blk', [(b, (b + by) % blocks) for b in range(block...  6.27 us
    select_n x2, other arithmetic, on_device(): jnp.where(uses_lifted, up_part, part)  3.81 us
  transfers between devices with their start and end apart: 18, of which 6 were waited for; matrix products, arithmetic and copies ran while one was open for 3% of the time, Pallas kernels for 30%

profile of v3, /device:TPU:1, one launch (start us, length us, event | category | flops | bytes accessed | tf_op | source)
XLA Modules:
  0.0 168.0 jit_solution(6489699375350672713)
XLA Ops:
  0.6 1.5 collective-permute-start.4
  2.1 1.3 collective-permute-start
  3.4 2.5 %collective-permute-start.1 = (s32[128]{0:T(128)}, s32[128]{0:T(128)S(1)}, u32[]{:S(2)}, u32[]{:S(2)}) collective-permute-start(s32[128]{0:T(128)} %param.5), channel_id=1, source_target_pairs={{0,8},{4,12},{8,16},{12,20},{16,24},{20,28},{24,32},{28,36},{32,40... | collective-permute-start | bytes 1544 | tf_op jit(solution)/shard_map/ppermute | solution.py:292
  5.9 2.5 %collective-permute-start.2 = (s32[128]{0:T(128)}, s32[128]{0:T(128)S(1)}, u32[]{:S(2)}, u32[]{:S(2)}) collective-permute-start(s32[128]{0:T(128)} %param.5), channel_id=1, source_target_pairs={{0,12},{4,16},{8,20},{12,24},{16,28},{20,32},{24,36},{28,40},{32,4... | collective-permute-start | bytes 1544 | tf_op jit(solution)/shard_map/ppermute | solution.py:292
  8.5 3.1 %shard_map.52 = bf16[128,5376]{1,0:T(8,128)(2,1)} custom-call(bf16[128,4,5376]{2,1,0:T(4,128)(2,1)} %source.2, s32[2]{0:T(128)S(1)} %pad_add_fusion.1.origin), custom_call_target="tpu_custom_call" | custom-call | tf_op jit(solution)/shard_map/pallas_call | solution.py:212
  11.6 1.1 collective-permute-start.6
  12.8 5.4 %shard_map.50 = (bf16[256,5376]{1,0:T(8,128)(2,1)}, bf16[128,5376]{1,0:T(8,128)(2,1)}, bf16[128,5376]{1,0:T(8,128)(2,1)}, bf16[128,5376]{1,0:T(8,128)(2,1)}) custom-call(bf16[128,4,5376]{2,1,0:T(4,128)(2,1)} %source.2, s32[5]{0:T(128)S(1)} %stack.21.origin), custom_call_target="tpu_custom_call" | custom-call | tf_op jit(solution)/shard_map/pallas_call | solution.py:212
  18.2 1.8 %collective-permute-start.9 = (bf16[128,5376]{1,0:T(8,128)(2,1)}, bf16[128,5376]{1,0:T(8,128)(2,1)}, u32[]{:S(2)}, u32[]{:S(2)}) collective-permute-start(bf16[128,5376]{1,0:T(8,128)(2,1)} %get-tuple-element.26), channel_id=1, source_target_pairs={{4,20},{6,22},{13,29},{15,31},{20,36},{22,38},{29,45},{31,47},{36,... | collective-permute-start | bytes 4128776 | tf_op jit(solution)/shard_map/ppermute | solution.py:259
  20.3 2.3 %collective-permute-start.3 = (bf16[128,5376]{1,0:T(8,128)(2,1)}, bf16[128,5376]{1,0:T(8,128)(2,1)}, u32[]{:S(2)}, u32[]{:S(2)}) collective-permute-start(bf16[128,5376]{1,0:T(8,128)(2,1)} %get-tuple-element.17), channel_id=1, source_target_pairs={{0,4},{1,13},{2,6},{3,15},{4,8},{5,17},{6,10},{7,19},{8,12},{9,21}... | collective-permute-start | bytes 4128776 | tf_op jit(solution)/shard_map/ppermute | solution.py:259
  22.6 0.9 collective-permute-start.11
  23.4 21.5 %collective-permute-done.6.refs_0_ = bf16[128,5376]{1,0:T(8,128)(2,1)S(1)} collective-permute-done((bf16[128,5376]{1,0:T(8,128)(2,1)}, bf16[128,5376]{1,0:T(8,128)(2,1)S(1)}, u32[]{:S(2)}, u32[]{:S(2)}) %collective-permute-start.6) | collective-permute-done | bytes 1376288 | tf_op jit(solution)/shard_map/ppermute | solution.py:259
  45.0 2.6 %broadcast_select_fusion.1 = bf16[128,5376]{1,0:T(8,128)(2,1)} fusion(bf16[128,5376]{1,0:T(8,128)(2,1)} %collective-permute-done.9, bf16[128,5376]{1,0:T(8,128)(2,1)} %get-tuple-element.26, pred[]{:T(512)S(6)} %eq.12), kind=kLoop, calls=%fused_computation.1 | loop fusion | flops 688128 | bytes 4128769 | tf_op jit(solution)/shard_map/jit(_where)/select_n | solution.py:320
  47.5 1.6 collective-permute-start.10
  49.3 10.3 %shard_map.51 = f32[8,256]{1,0:T(8,128)S(1)} custom-call(bf16[256,5376]{1,0:T(8,128)(2,1)S(1)} %copy-done, s32[1]{0:T(128)} %constant.88.clone.1.refs_1_, bf16[1024,5376]{1,0:T(8,128)(2,1)} %refs_5_.1, bf16[1024,5376]{1,0:T(8,128)(2,1)} %collective-permute-done.4.refs_3_.refs_4_.refs_6_, s32[256,128]{1,0:T(8,128)S(1)} %broadcast_in_dim.101.refs_4_), custom_call_target="tpu_custom_call" | custom-call | tf_op jit(solution)/shard_map/pallas_call | solution.py:148
  59.6 13.2 %collective-permute-done.3.refs_1_ = bf16[128,5376]{1,0:T(8,128)(2,1)} collective-permute-done((bf16[128,5376]{1,0:T(8,128)(2,1)}, bf16[128,5376]{1,0:T(8,128)(2,1)}, u32[]{:S(2)}, u32[]{:S(2)}) %collective-permute-start.3) | collective-permute-done | bytes 1376288 | tf_op jit(solution)/shard_map/ppermute | solution.py:259
  72.8 1.2 broadcast_select_fusion
  74.0 5.2 %collective-permute-start.12 = (bf16[128,5376]{1,0:T(8,128)(2,1)}, bf16[128,5376]{1,0:T(8,128)(2,1)}, u32[]{:S(2)}, u32[]{:S(2)}) collective-permute-start(bf16[128,5376]{1,0:T(8,128)(2,1)} %broadcast_select_fusion), channel_id=1, source_target_pairs={{0,12},{1,5},{2,14},{3,7},{4,0},{5,9},{6,2},{7,11},{8,20},{9,13},{... | collective-permute-start | bytes 4128776 | tf_op jit(solution)/shard_map/ppermute | solution.py:259
  79.7 12.0 %shard_map.53 = f32[8,256]{1,0:T(8,128)S(1)} custom-call(bf16[128,5376]{1,0:T(8,128)(2,1)S(1)} %collective-permute-done.6.refs_0_, bf16[128,5376]{1,0:T(8,128)(2,1)} %collective-permute-done.3.refs_1_, s32[2]{0:T(128)S(1)} %iota_multiply_fusion.1.refs_2_, bf16[1024,5376]{1,0:T(8,128)(2,1)} %refs_5_.1, ...), custom_call_target="tpu_custom_call" | custom-call | tf_op jit(solution)/shard_map/pallas_call | solution.py:148
  91.7 40.5 %collective-permute-done.5.refs_1_ = bf16[128,5376]{1,0:T(8,128)(2,1)} collective-permute-done((bf16[128,5376]{1,0:T(8,128)(2,1)}, bf16[128,5376]{1,0:T(8,128)(2,1)}, u32[]{:S(2)}, u32[]{:S(2)}) %collective-permute-start.5) | collective-permute-done | bytes 1376288 | tf_op jit(solution)/shard_map/ppermute | solution.py:259
  132.3 19.9 %shard_map.54 = (f32[8,256]{1,0:T(8,128)S(1)}, f32[8,256]{1,0:T(8,128)S(1)}) custom-call(bf16[128,5376]{1,0:T(8,128)(2,1)S(1)} %collective-permute-done.8.refs_0_, bf16[128,5376]{1,0:T(8,128)(2,1)} %collective-permute-done.5.refs_1_, bf16[128,5376]{1,0:T(8,128)(2,1)} %collective-permute-done.10.refs_2_, bf16[128,5376]{1,0:T(8,128)(2,1)} %collective-permute-done.12.refs_3_, ...), custom_call_target="tpu_custom_call" | custom-call | tf_op jit(solution)/shard_map/pallas_call | solution.py:148
  152.2 1.5 collective-permute-start.14
  153.7 1.1 collective-permute-done.14
  154.8 2.9 %collective-permute-done.13 = f32[8,256]{1,0:T(8,128)S(1)} collective-permute-done((f32[8,256]{1,0:T(8,128)S(1)}, f32[8,256]{1,0:T(8,128)S(1)}, u32[]{:S(2)}, u32[]{:S(2)}) %collective-permute-start.13) | collective-permute-done | bytes 8224 | tf_op jit(solution)/shard_map/ppermute | solution.py:259
  158.2 0.3 fusion.10
  159.8 0.4 collective-permute-start.17
  160.2 3.0 %collective-permute-start.15 = (f32[4,256]{1,0:T(4,128)S(1)}, f32[4,256]{1,0:T(4,128)S(1)}, u32[]{:S(2)}, u32[]{:S(2)}) collective-permute-start(f32[4,256]{1,0:T(4,128)S(1)} %pad_maximum_fusion), channel_id=1, source_target_pairs={{0,2},{1,3},{2,0},{3,1},{4,6},{5,7},{6,4},{7,5},{8,10},{9,11},{10,... | collective-permute-start | bytes 12296 | tf_op jit(solution)/shard_map/ppermute | solution.py:259
  163.3 1.1 collective-permute-done.17
  164.5 0.2 fusion.4
  165.3 0.2 exponential_reduce_fusion
  166.3 0.7 copy.26
  167.1 0.2 slice_reduce_fusion
  167.4 0.7 copy.27
  (83 shorter events, 4.4 us)
Async XLA Ops:
  0.6 48.5 %collective-permute-start.4 = (bf16[1024,5376]{1,0:T(8,128)(2,1)}, bf16[1024,5376]{1,0:T(8,128)(2,1)}, u32[]{:S(2)}, u32[]{:S(2)}) collective-permute-start(bf16[1024,5376]{1,0:T(8,128)(2,1)} %refs_5_.1), channel_id=1, source_target_pairs={{0,1},{1,0},{2,3},{3,2},{4,5},{5,4},{6,7},{7,6},{8,9},{9,8},{10,11... | collective-permute-start | bytes 33030152 | tf_op jit(solution)/shard_map/ppermute | solution.py:259
  2.1 10.6 %collective-permute-start = (s32[128]{0:T(128)}, s32[128]{0:T(128)S(1)}, u32[]{:S(2)}, u32[]{:S(2)}) collective-permute-start(s32[128]{0:T(128)} %param.5), channel_id=1, source_target_pairs={{0,4},{4,8},{8,12},{12,16},{16,20},{20,24},{24,28},{28,32},{32,36}... | collective-permute-start | bytes 1544 | tf_op jit(solution)/shard_map/ppermute | solution.py:292
  3.4 9.3 %collective-permute-start.1 = (s32[128]{0:T(128)}, s32[128]{0:T(128)S(1)}, u32[]{:S(2)}, u32[]{:S(2)}) collective-permute-start(s32[128]{0:T(128)} %param.5), channel_id=1, source_target_pairs={{0,8},{4,12},{8,16},{12,20},{16,24},{20,28},{24,32},{28,36},{32,40... | collective-permute-start | bytes 1544 | tf_op jit(solution)/shard_map/ppermute | solution.py:292
  5.9 6.9 %collective-permute-start.2 = (s32[128]{0:T(128)}, s32[128]{0:T(128)S(1)}, u32[]{:S(2)}, u32[]{:S(2)}) collective-permute-start(s32[128]{0:T(128)} %param.5), channel_id=1, source_target_pairs={{0,12},{4,16},{8,20},{12,24},{16,28},{20,32},{24,36},{28,40},{32,4... | collective-permute-start | bytes 1544 | tf_op jit(solution)/shard_map/ppermute | solution.py:292
  11.6 33.3 %collective-permute-start.6 = (bf16[128,5376]{1,0:T(8,128)(2,1)}, bf16[128,5376]{1,0:T(8,128)(2,1)S(1)}, u32[]{:S(2)}, u32[]{:S(2)}) collective-permute-start(bf16[128,5376]{1,0:T(8,128)(2,1)} %shard_map.52), channel_id=1, source_target_pairs={{0,4},{1,13},{2,6},{3,15},{4,8},{5,17},{6,10},{7,19},{8,12},{9,21}... | collective-permute-start | bytes 4128776 | tf_op jit(solution)/shard_map/ppermute | solution.py:259
  12.8 7.2 %copy-start.2 = (s32[128]{0:T(128)S(1)}, s32[128]{0:T(128)}, u32[]{:S(2)}) copy-start(s32[128]{0:T(128)} %param.5) | copy-start | bytes 1540
  18.2 26.7 %collective-permute-start.9 = (bf16[128,5376]{1,0:T(8,128)(2,1)}, bf16[128,5376]{1,0:T(8,128)(2,1)}, u32[]{:S(2)}, u32[]{:S(2)}) collective-permute-start(bf16[128,5376]{1,0:T(8,128)(2,1)} %get-tuple-element.26), channel_id=1, source_target_pairs={{4,20},{6,22},{13,29},{15,31},{20,36},{22,38},{29,45},{31,47},{36,... | collective-permute-start | bytes 4128776 | tf_op jit(solution)/shard_map/ppermute | solution.py:259
  20.3 52.5 %collective-permute-start.3 = (bf16[128,5376]{1,0:T(8,128)(2,1)}, bf16[128,5376]{1,0:T(8,128)(2,1)}, u32[]{:S(2)}, u32[]{:S(2)}) collective-permute-start(bf16[128,5376]{1,0:T(8,128)(2,1)} %get-tuple-element.17), channel_id=1, source_target_pairs={{0,4},{1,13},{2,6},{3,15},{4,8},{5,17},{6,10},{7,19},{8,12},{9,21}... | collective-permute-start | bytes 4128776 | tf_op jit(solution)/shard_map/ppermute | solution.py:259
  22.6 26.7 %copy-start = (bf16[256,5376]{1,0:T(8,128)(2,1)S(1)}, bf16[256,5376]{1,0:T(8,128)(2,1)}, u32[]{:S(2)}) copy-start(bf16[256,5376]{1,0:T(8,128)(2,1)} %get-tuple-element.18.refs_0_) | copy-start | bytes 8257540
  22.6 50.2 %collective-permute-start.11 = (bf16[128,5376]{1,0:T(8,128)(2,1)}, bf16[128,5376]{1,0:T(8,128)(2,1)S(1)}, u32[]{:S(2)}, u32[]{:S(2)}) collective-permute-start(bf16[128,5376]{1,0:T(8,128)(2,1)} %get-tuple-element.27), channel_id=1, source_target_pairs={{4,20},{6,22},{13,29},{15,31},{20,36},{22,38},{29,45},{31,47},{36,... | collective-permute-start | bytes 4128776 | tf_op jit(solution)/shard_map/ppermute | solution.py:259
  44.9 87.3 %collective-permute-start.8 = (bf16[128,5376]{1,0:T(8,128)(2,1)S(1)}, bf16[128,5376]{1,0:T(8,128)(2,1)S(1)}, u32[]{:S(2)}, u32[]{:S(2)}) collective-permute-start(bf16[128,5376]{1,0:T(8,128)(2,1)S(1)} %collective-permute-done.6.refs_0_), channel_id=1, source_target_pairs={{0,4},{1,125},{2,6},{3,127},{4,8},{5,1},{6,10},{7,3},{8,12},{9,5},... | collective-permute-start | bytes 4128776 | tf_op jit(solution)/shard_map/ppermute | solution.py:259
  47.5 84.8 %collective-permute-start.10 = (bf16[128,5376]{1,0:T(8,128)(2,1)}, bf16[128,5376]{1,0:T(8,128)(2,1)}, u32[]{:S(2)}, u32[]{:S(2)}) collective-permute-start(bf16[128,5376]{1,0:T(8,128)(2,1)} %broadcast_select_fusion.1), channel_id=1, source_target_pairs={{0,12},{1,5},{2,14},{3,7},{4,0},{5,9},{6,2},{7,11},{8,20},{9,13},{... | collective-permute-start | bytes 4128776 | tf_op jit(solution)/shard_map/ppermute | solution.py:259
  49.3 23.5 %copy-start.1 = (bf16[128,5376]{1,0:T(8,128)(2,1)S(1)}, bf16[128,5376]{1,0:T(8,128)(2,1)}, u32[]{:S(2)}) copy-start(bf16[128,5376]{1,0:T(8,128)(2,1)} %get-tuple-element.27) | copy-start | bytes 4128772
  72.8 59.5 %collective-permute-start.5 = (bf16[128,5376]{1,0:T(8,128)(2,1)}, bf16[128,5376]{1,0:T(8,128)(2,1)}, u32[]{:S(2)}, u32[]{:S(2)}) collective-permute-start(bf16[128,5376]{1,0:T(8,128)(2,1)} %collective-permute-done.3.refs_1_), channel_id=1, source_target_pairs={{0,4},{1,125},{2,6},{3,127},{4,8},{5,1},{6,10},{7,3},{8,12},{9,5},... | collective-permute-start | bytes 4128776 | tf_op jit(solution)/shard_map/ppermute | solution.py:259
  74.0 58.2 %collective-permute-start.12 = (bf16[128,5376]{1,0:T(8,128)(2,1)}, bf16[128,5376]{1,0:T(8,128)(2,1)}, u32[]{:S(2)}, u32[]{:S(2)}) collective-permute-start(bf16[128,5376]{1,0:T(8,128)(2,1)} %broadcast_select_fusion), channel_id=1, source_target_pairs={{0,12},{1,5},{2,14},{3,7},{4,0},{5,9},{6,2},{7,11},{8,20},{9,13},{... | collective-permute-start | bytes 4128776 | tf_op jit(solution)/shard_map/ppermute | solution.py:259
  132.3 21.4 %collective-permute-start.7 = (f32[8,256]{1,0:T(8,128)S(1)}, f32[8,256]{1,0:T(8,128)S(1)}, u32[]{:S(2)}, u32[]{:S(2)}) collective-permute-start(f32[8,256]{1,0:T(8,128)S(1)} %shard_map.53), channel_id=1, source_target_pairs={{0,124},{1,117},{2,126},{3,119},{4,0},{5,121},{6,2},{7,123},{8,4},... | collective-permute-start | bytes 24584 | tf_op jit(solution)/shard_map/ppermute | solution.py:259
  152.2 2.6 %collective-permute-start.14 = (f32[8,256]{1,0:T(8,128)S(1)}, f32[8,256]{1,0:T(8,128)S(1)}, u32[]{:S(2)}, u32[]{:S(2)}) collective-permute-start(f32[8,256]{1,0:T(8,128)S(1)} %get-tuple-element.29), channel_id=1, source_target_pairs={{0,116},{1,125},{2,118},{3,127},{4,120},{5,1},{6,122},{7,3},{8,124... | collective-permute-start | bytes 24584 | tf_op jit(solution)/shard_map/ppermute | solution.py:259
  153.7 4.0 %collective-permute-start.13 = (f32[8,256]{1,0:T(8,128)S(1)}, f32[8,256]{1,0:T(8,128)S(1)}, u32[]{:S(2)}, u32[]{:S(2)}) collective-permute-start(f32[8,256]{1,0:T(8,128)S(1)} %get-tuple-element.28), channel_id=1, source_target_pairs={{0,120},{1,121},{2,122},{3,123},{4,124},{5,125},{6,126},{7,127},{8... | collective-permute-start | bytes 24584 | tf_op jit(solution)/shard_map/ppermute | solution.py:259
  159.7 3.5 %collective-permute-start.16 = (f32[4,256]{1,0:T(4,128)S(1)}, f32[4,256]{1,0:T(4,128)S(1)}, u32[]{:S(2)}, u32[]{:S(2)}) collective-permute-start(f32[4,256]{1,0:T(4,128)S(1)} %pad_maximum_fusion), channel_id=1, source_target_pairs={{0,1},{1,0},{2,3},{3,2},{4,5},{5,4},{6,7},{7,6},{8,9},{9,8},{10,11... | collective-permute-start | bytes 12296 | tf_op jit(solution)/shard_map/ppermute | solution.py:259
  159.8 4.6 %collective-permute-start.17 = (f32[4,256]{1,0:T(4,128)S(1)}, f32[4,256]{1,0:T(4,128)S(1)}, u32[]{:S(2)}, u32[]{:S(2)}) collective-permute-start(f32[4,256]{1,0:T(4,128)S(1)} %pad_maximum_fusion), channel_id=1, source_target_pairs={{0,3},{1,2},{2,1},{3,0},{4,7},{5,6},{6,5},{7,4},{8,11},{9,10},{10,... | collective-permute-start | bytes 12296 | tf_op jit(solution)/shard_map/ppermute | solution.py:259
  160.2 5.0 %collective-permute-start.15 = (f32[4,256]{1,0:T(4,128)S(1)}, f32[4,256]{1,0:T(4,128)S(1)}, u32[]{:S(2)}, u32[]{:S(2)}) collective-permute-start(f32[4,256]{1,0:T(4,128)S(1)} %pad_maximum_fusion), channel_id=1, source_target_pairs={{0,2},{1,3},{2,0},{3,1},{4,6},{5,7},{6,4},{7,5},{8,10},{9,11},{10,... | collective-permute-start | bytes 12296 | tf_op jit(solution)/shard_map/ppermute | solution.py:259
